TPU v7x, 256 devices: a whole 4x4x8 slice. The times are simulated.
256 devices in a mesh: dp: 8 (over x, core), proto: 32 (over y, z).
Axes of the slice: x: 4, y: 4, z: 8, core: 2. Of those that a mesh axis runs over, the one named last changes fastest.
Arguments:
- student_patches: bfloat16 [8192, 256], P('dp'), may hold values from -160 to 160
- teacher_patches: bfloat16 [8192, 256], P('dp'), may hold values from -160 to 160
- masked_index: int32 [32, 128], P('dp'), may hold values from 0 to 255, as said below
- prototypes: bfloat16 [256, 131072], P(None, 'proto'), may hold values from -2.5 to 2.5
Outputs:
- grad_patches: float32 [8192, 256], P('dp')
- grad_prototypes: float32 [256, 131072], P('dp', 'proto')
Inputs may be any that keep to these rules, and one draw needn't show every extreme that they name: `masked_index`: each row holds 128 distinct patch positions of its image.
All inputs are finite; a program needn't handle non-finite values.
Results may differ from a plain program's by a relative error of at most 0.0024.
Values sent between devices are 32-bit elements; how exact they have to be, the bound alone decides.
A program may use at most 64 MiB of HBM per device.

v0:
```python
import jax
import jax.numpy as jnp
from jax import lax
from jax.sharding import PartitionSpec as P

ITERS = 3


teacher_temp = 0.07
student_temp = 0.1
loss_factor = 4096.0
epsilon = 1e-06


def unit_rows(values):
    norms = jnp.sqrt(jnp.sum(values * values, axis=-1, keepdims=True) + epsilon)
    return (values / norms, norms)


def contract_rows(left, right):
    return lax.dot_general(
        left,
        right,
        (((0,), (0,)), ((), ())),
        precision=lax.Precision.HIGHEST,
        preferred_element_type=jnp.float32,
    )


def contract_cols(left, right):
    return lax.dot_general(
        left,
        right,
        (((1,), (1,)), ((), ())),
        precision=lax.Precision.HIGHEST,
        preferred_element_type=jnp.float32,
    )


def body(student_patches, teacher_patches, masked_index, prototypes):
    images, masked = masked_index.shape
    patch_count = student_patches.shape[0] // images
    row_count = images * masked
    offsets = patch_count * jnp.arange(images, dtype=jnp.int32)
    positions = (masked_index + offsets[:, None]).reshape(row_count)
    student = jnp.take(student_patches, positions, axis=0).astype(jnp.float32)
    teacher = jnp.take(teacher_patches, positions, axis=0).astype(jnp.float32)
    student_unit, student_norm = unit_rows(student)
    student_cast = student_unit.astype(jnp.bfloat16)
    teacher_cast = unit_rows(teacher)[0].astype(jnp.bfloat16)
    weights = prototypes.astype(jnp.float32)
    proto_norm = jnp.sqrt(jnp.sum(weights * weights, axis=0) + epsilon)
    proto_unit = weights / proto_norm[None, :]
    proto_cast = proto_unit.astype(jnp.bfloat16)
    expos = jnp.exp(
        jnp.dot(teacher_cast, proto_cast, preferred_element_type=jnp.float32) / teacher_temp
    )
    target = expos
    for sweep in range(ITERS):
        target = target / lax.psum(jnp.sum(target, axis=0), "dp")[None, :]
        target = target / lax.psum(jnp.sum(target, axis=1), "proto")[:, None]
    student_exp = jnp.exp(
        jnp.dot(student_cast, proto_cast, preferred_element_type=jnp.float32) / student_temp
    )
    totals = lax.psum(jnp.sum(student_exp, axis=1), "proto")
    slopes = loss_factor / student_temp * (student_exp / totals[:, None] - target)
    grad_unit = lax.psum(contract_cols(slopes, proto_unit), "proto")
    grad_rows = (
        grad_unit - student_unit * jnp.sum(student_unit * grad_unit, axis=-1, keepdims=True)
    ) / student_norm
    grad_patches = (
        jnp.zeros((student_patches.shape[0], student_patches.shape[1]), jnp.float32)
        .at[positions]
        .set(grad_rows)
    )
    share_width = weights.shape[0] // lax.axis_size("dp")
    first_width = lax.axis_index("dp") * share_width
    weight_total = lax.psum(contract_rows(student_unit, slopes), "dp")
    inner_dot = jnp.sum(proto_unit * weight_total, axis=0)
    grad_full = (weight_total - proto_unit * inner_dot[None, :]) / proto_norm[None, :]
    grad_prototypes = lax.dynamic_slice_in_dim(grad_full, first_width, share_width, 0)
    return (grad_patches, grad_prototypes)


def solution(mesh):
    placed = (P("dp", None), P("dp", None), P("dp", None), P(None, "proto"))
    return jax.shard_map(
        body,
        mesh=mesh,
        in_specs=placed,
        out_specs=(P("dp", None), P("dp", "proto")),
        check_vma=False,
    )
```

profile of v0, /device:TPU:1, one launch (start us, length us, event | category | flops | bytes accessed | tf_op | source)
XLA Modules:
  0.0 585.4 jit_solution(15430623845415431041)
XLA Ops:
  7.2 0.0 all-reduce.4.cloned.1.call-start
  7.2 0.8 compare_and_fusion
  8.1 0.2 copy-done
  8.2 1.9 gather_fusion
  10.2 2.7 gather_fusion.1
  12.9 2.0 fusion.14
  14.9 0.3 fusion.18
  15.3 6.1 %fusion.35 = (f32[4096]{0:T(1024)S(1)}, f32[512,4096]{1,0:T(8,128)}) fusion(f32[4096]{0:T(1024)S(1)} %add_sqrt_fusion, bf16[256,4096]{1,0:T(8,128)(2,1)} %param.9, f32[512]{0:T(512)S(1)} %get-tuple-element.15, bf16[512,256]{1,0:T(8,128)(2,1)S(1)} %gather_fusion.1, pred[512]{0:T(512)(128)(4,1)S(1)} %get-tuple-element.7), kind=kOutput, calls=%fused_computation.63 | convolution fusion | flops 1081602048 | bytes 10783232 | tf_op jit(solution)/shard_map/dot_general | solution.py:56
  21.4 23.6 %psum.64 = f32[4096]{0:T(1024)S(1)} all-reduce(f32[4096]{0:T(1024)S(1)} %get-tuple-element.11), channel_id=1, replica_groups=mesh['dp'=8,'proto'=32] {'dp'}, use_global_device_ids=true, to_apply=%region_6.8 | all-reduce | flops 4096 | bytes 32768 | tf_op jit(solution)/shard_map/psum | solution.py:60
  44.9 4.0 divide_reduce_fusion
  49.0 64.1 %psum.65 = f32[512]{0:T(512)S(1)} all-reduce(f32[512]{0:T(512)S(1)} %divide_reduce_fusion), channel_id=1, replica_groups=mesh['dp'=8,'proto'=32] {'proto'}, use_global_device_ids=true, to_apply=%region_8.10 | all-reduce | flops 512 | bytes 4096 | tf_op jit(solution)/shard_map/psum | solution.py:61
  113.0 4.7 fusion.9
  117.7 37.4 %psum.66 = f32[4096]{0:T(1024)S(1)} all-reduce(f32[4096]{0:T(1024)S(1)} %fusion.9), channel_id=1, replica_groups=mesh['dp'=8,'proto'=32] {'dp'}, use_global_device_ids=true, to_apply=%region_10.12 | all-reduce | flops 4096 | bytes 32768 | tf_op jit(solution)/shard_map/psum | solution.py:60
  155.2 4.3 fusion.10
  159.5 55.8 %psum.67 = f32[512]{0:T(512)S(1)} all-reduce(f32[512]{0:T(512)S(1)} %fusion.10), channel_id=1, replica_groups=mesh['dp'=8,'proto'=32] {'proto'}, use_global_device_ids=true, to_apply=%region_12.14 | all-reduce | flops 512 | bytes 4096 | tf_op jit(solution)/shard_map/psum | solution.py:61
  215.2 4.6 fusion.11
  219.8 37.4 %psum.68 = f32[4096]{0:T(1024)S(1)} all-reduce(f32[4096]{0:T(1024)S(1)} %fusion.11), channel_id=1, replica_groups=mesh['dp'=8,'proto'=32] {'dp'}, use_global_device_ids=true, to_apply=%region_14.16 | all-reduce | flops 4096 | bytes 32768 | tf_op jit(solution)/shard_map/psum | solution.py:60
  257.3 4.6 fusion.12
  261.9 4.4 fusion.13
  266.3 57.9 %all-reduce = (f32[512]{0:T(512)S(1)}, f32[512]{0:T(512)S(1)}) all-reduce(f32[512]{0:T(512)S(1)} %fusion.12, f32[512]{0:T(512)S(1)} %get-tuple-element.13), channel_id=1, replica_groups=mesh['dp'=8,'proto'=32] {'proto'}, use_global_device_ids=true, to_apply=%region_16.18 | all-reduce | flops 1024 | bytes 8192 | tf_op jit(solution)/shard_map/psum | solution.py:61
  324.2 8.0 %fusion.8 = f32[512,4096]{1,0:T(8,128)S(1)} fusion(f32[512,4096]{1,0:T(8,128)} %get-tuple-element.12, f32[512,4096]{1,0:T(8,128)} %get-tuple-element.14, f32[512]{0:T(512)S(1)} %get-tuple-element.5, f32[4096]{0:T(1024)S(1)} %psum.68, f32[512]{0:T(512)S(1)} %psum.67, f32[4096]{0:T(1024)S(1)} %psum.66, f32[512]{0:T(512)S(1)} %psum.65, f32[4096]{0:T(1024)S(1)} %psum.64, ...), kind=kLoop, calls=%fused_computation.13 | loop fusion | flops 20971520 | bytes 25223168 | tf_op jit(solution)/shard_map/mul | solution.py:66
  332.2 3.2 copy-done.1
  335.5 7.6 %fusion.34 = f32[512,256]{1,0:T(8,128)} fusion(f32[512,4096]{1,0:T(8,128)S(1)} %fusion.8, bf16[256,4096]{1,0:T(8,128)(2,1)S(1)} %copy-done.2, f32[4096]{0:T(1024)S(1)} %add_sqrt_fusion), kind=kOutput, calls=%fused_computation.62 | convolution fusion | flops 6444548096 | bytes 11026432 | tf_op jit(solution)/shard_map/dot_general | solution.py:31
  343.1 0.0 all-reduce.4.cloned.1.call-update
  343.1 0.3 all-reduce.6.cloned.1.call-start
  343.4 11.2 %fusion.33 = f32[256,4096]{1,0:T(8,128)} fusion(f32[512,4096]{1,0:T(8,128)} %copy-done.1, f32[512]{0:T(512)S(1)} %get-tuple-element.16, bf16[512,256]{1,0:T(8,128)(2,1)S(1)} %gather_fusion, pred[512]{0:T(512)(128)(4,1)S(1)} %get-tuple-element.7), kind=kOutput, calls=%fused_computation.61 | convolution fusion | flops 6442844160 | bytes 12847616 | tf_op jit(solution)/shard_map/dot_general | solution.py:21
  354.6 139.3 %all-reduce.4.cloned.1.call-done = f32[512,256]{1,0:T(8,128)} async-done(((f32[512,256]{1,0:T(8,128)}), f32[512,256]{1,0:T(8,128)}) %all-reduce.4.cloned.1.call-update) | async-done | bytes 524304 | tf_op jit(solution)/shard_map/psum | solution.py:67
  493.8 1.3 multiply_reduce_fusion.1
  495.2 4.0 scatter_custom_fusion
  499.2 74.5 %all-reduce.6.cloned.1.call-done = f32[256,4096]{1,0:T(8,128)} async-done(((f32[256,4096]{1,0:T(8,128)}), f32[256,4096]{1,0:T(8,128)}) %all-reduce.6.cloned.1.call-update) | async-done | bytes 4194320 | tf_op jit(solution)/shard_map/psum | solution.py:78
  573.7 3.0 multiply_reduce_fusion
  576.6 1.9 fusion.21
  (11 shorter events, 0.1 us)
Async XLA Ops:
  7.2 1.1 copy-start
  7.2 486.6 %all-reduce.4.cloned.1.call-start = ((), (), s32[]{:S(2)}) async-start(), calls=%async_computation | async-start | bytes 1048576 | tf_op jit(solution)/shard_map/psum | solution.py:67
  215.2 46.6 %copy-start.2 = (bf16[256,4096]{1,0:T(8,128)(2,1)S(1)}, bf16[256,4096]{1,0:T(8,128)(2,1)}, u32[]{:S(2)}) copy-start(bf16[256,4096]{1,0:T(8,128)(2,1)} %param.9) | copy-start | bytes 6291460
  332.2 3.2 copy-start.1
  343.1 230.6 %all-reduce.6.cloned.1.call-start = ((), (), s32[]{:S(2)}) async-start(), calls=%async_computation.1 | async-start | bytes 8388608 | tf_op jit(solution)/shard_map/psum | solution.py:78
Sparse Core Ops, SparseCore 0:
  343.2 150.5 all-reduce.3
  496.3 77.2 all-reduce.5
where the time goes:
time: 587 us; the launch traced here: 585 us
  blocking collectives  276 us (47%)
  waiting for transfers between devices  214 us (36%)
  other arithmetic  43.7 us (7%)
  matrix products  29.3 us (5%)
  between operations  14.1 us (2%)
  local copies, waits for them, and re-layouts  8.02 us (1%)
    psum x3, blocking collectives, body(): target = target / lax.psum(jnp.sum(target, axis=1), 'proto')[:, None]  178 us
    psum x1, waiting for transfers between devices, body(): grad_unit = lax.psum(contract_cols(slopes, proto_unit), 'proto')  139 us
    psum x3, blocking collectives, body(): target = target / lax.psum(jnp.sum(target, axis=0), 'dp')[None, :]  98.4 us
    psum x1, waiting for transfers between devices, body(): weight_total = lax.psum(contract_rows(student_unit, slopes), 'dp')  74.5 us
    reduce_sum x3, other arithmetic, body(): target = target / lax.psum(jnp.sum(target, axis=1), 'proto')[:, None]  12.9 us
  transfers between devices with their start and end apart: 2, of which 2 were waited for; matrix products, arithmetic and copies ran while one was open for 3% of the time, Pallas kernels for 0%

commit v1 on v0

v1 whole, which is shorter than its diff:
```python
import math

import jax
import jax.numpy as jnp
from jax import lax
from jax.experimental import pallas as pl
from jax.experimental.pallas import tpu as pltpu
from jax.sharding import PartitionSpec as P

MESH = pl.DeviceIdType.MESH
F32 = jnp.float32
BF16 = jnp.bfloat16

teacher_scale = math.log2(math.e) / 0.07
student_scale = math.log2(math.e) / 0.1
slope_scale = 4096.0 / 0.1
epsilon = 1e-06

W = 512
NY, NZ = 4, 8
FAR_FIRST = sorted(
    [(dy, dz) for dy in range(NY) for dz in range(NZ) if dy or dz],
    key=lambda o: -(min(o[0], NY - o[0]) + min(o[1], NZ - o[1])),
)


def dot(a, b):
    return jnp.dot(a, b, preferred_element_type=F32)


def dot_cols(a, b):
    return lax.dot_general(a, b, (((1,), (1,)), ((), ())), preferred_element_type=F32)


def split(value):
    high = value.astype(BF16)
    return high, (value - high.astype(F32)).astype(BF16)


def kernel(
    student_hbm, teacher_hbm, index_hbm, protos_hbm,
    gp_ref, gw_ref,
    student_v, teacher_v, index_v, protos_v, in_sem,
    onehot, t_send, s_send, t_other, s_other, t_cast, s_cast, s_unit_t, s_inv,
    pc, plo, pinv, expos,
    e2h, e2l, x2h, x2l, wtp, a_hi, a_lo,
    cbuf, c_ssem, c_rsem,
    r1buf, r2buf, r3buf, r_ssem, r_rsem, ub, vrow, tot_row, tot_acc, totb,
    ts_ssem, ts_rsem, swap_s, swap_r, swap_ssem, swap_rsem,
    fp, ft, yr, ysum, y_ssem, y_rsem, zr, z_ssem, z_rsem,
    ag, agz_ssem, agz_rsem, agy_ssem, agy_rsem,
    gpart, p1r, p1_ssem, p1_rsem, p2r, p2_ssem, p2_rsem,
    fin_s, fin_r, fin_ssem, fin_rsem,
):
    dp = lax.axis_index("dp")
    pr = lax.axis_index("proto")
    x, core = lax.div(dp, 2), lax.rem(dp, 2)
    y, z = lax.div(pr, NZ), lax.rem(pr, NZ)
    x_next, x_prev, x_far = lax.rem(x + 1, 4), lax.rem(x + 3, 4), lax.rem(x + 2, 4)
    right = (x_next * 2 + core, pr)
    left = (x_prev * 2 + core, pr)
    partner = (x * 2 + 1 - core, pr)

    def dp_peer(k):
        return (lax.rem(dp + k, 8), pr)

    def proto_peer(dy, dz):
        return (dp, lax.rem(y + dy, NY) * NZ + lax.rem(z + dz, NZ))

    def remote(src, dst, ssem, rsem, device):
        return pltpu.make_async_remote_copy(
            src, dst, ssem, rsem, device_id=device, device_id_type=MESH
        )

    def wait_bytes(ref, sem):
        pltpu.make_async_copy(ref, ref, sem).wait()

    barrier = pltpu.get_barrier_semaphore()
    for k in range(1, 8):
        pl.semaphore_signal(barrier, inc=1, device_id=dp_peer(k), device_id_type=MESH)
    for dy, dz in FAR_FIRST:
        pl.semaphore_signal(
            barrier, inc=1, device_id=proto_peer(dy, dz), device_id_type=MESH
        )
    loads = [
        pltpu.make_async_copy(src, dst, in_sem.at[i])
        for i, (src, dst) in enumerate(
            [(index_hbm, index_v), (teacher_hbm, teacher_v), (protos_hbm, protos_v), (student_hbm, student_v)]
        )
    ]
    for load in loads:
        load.start()

    loads[0].wait()
    for i in range(4):
        places = lax.broadcasted_iota(jnp.int32, (256, 128), 0)
        onehot[i] = jnp.where(places == index_v[i : i + 1, :], 1.0, 0.0).astype(BF16)

    def masked(patches, i):
        rows = lax.dot_general(
            onehot[i], patches[256 * i : 256 * i + 256, :],
            (((0,), (0,)), ((), ())), preferred_element_type=F32,
        )
        norm = jnp.sqrt(jnp.sum(rows * rows, axis=1, keepdims=True) + epsilon)
        return rows / norm, norm

    loads[1].wait()
    for i in range(4):
        unit, _ = masked(teacher_v, i)
        t_send[128 * i : 128 * i + 128, :] = unit
        t_cast[128 * i : 128 * i + 128, :] = unit.astype(BF16)

    def put_cols(buf, slot, j, sums):
        for q in range(W // 128):
            buf[slot, pl.ds(4 * j + q, 1), :] = sums[:, 128 * q : 128 * q + 128]

    loads[2].wait()

    def front(j, carry):
        cols = pl.ds(pl.multiple_of(j * W, W), W)
        weights = protos_v[:, cols].astype(F32)
        inv = 1.0 / jnp.sqrt(jnp.sum(weights * weights, axis=0, keepdims=True) + epsilon)
        pinv[:, cols] = inv
        high, low = split(weights * inv)
        pc[:, cols] = high
        plo[:, cols] = low
        block = jnp.exp2(dot(t_cast[...], high) * teacher_scale)
        expos[:, cols] = block
        put_cols(cbuf.at[0], dp, j, jnp.sum(block, axis=0, keepdims=True))
        return carry

    lax.fori_loop(0, 8, front, 0)
    pl.semaphore_wait(barrier, 7 + len(FAR_FIRST))

    def send_cols(t):
        for k in (4, 3, 5, 2, 6, 1, 7):
            remote(cbuf.at[t, dp], cbuf.at[t, dp], c_ssem.at[t], c_rsem.at[t], dp_peer(k)).start()

    def take_cols(t):
        wait_bytes(cbuf.at[t, pl.ds(0, 7)], c_rsem.at[t])
        vrow[...] = 1.0 / jnp.sum(cbuf[t], axis=0)

    def send_rows(buf, t):
        for dy, dz in FAR_FIRST:
            remote(buf.at[pr], buf.at[pr], r_ssem.at[t], r_rsem.at[t], proto_peer(dy, dz)).start()

    def take_rows(buf, t):
        wait_bytes(buf.at[pl.ds(0, 31)], r_rsem.at[t])
        return jnp.sum(buf[...], axis=0)

    def spread(row):
        return jnp.transpose(jnp.broadcast_to(row, (128, 128)))

    def row_pass(buf):
        def image(i, carry):
            rows = pl.ds(pl.multiple_of(i * 128, 128), 128)
            total = expos[rows, 0:128] * vrow[0:1, :]
            for k in range(1, 32):
                total += expos[rows, 128 * k : 128 * k + 128] * vrow[k : k + 1, :]
            buf[pr, pl.ds(i, 1), :] = jnp.sum(jnp.transpose(total), axis=0, keepdims=True)
            return carry

        lax.fori_loop(0, 4, image, 0)

    def col_pass(t):
        def chunk(k, carry):
            cols = pl.ds(pl.multiple_of(k * 128, 128), 128)
            cbuf[t, dp, pl.ds(k, 1), :] = jnp.sum(
                expos[:, cols] * ub[...], axis=0, keepdims=True
            )
            return carry

        lax.fori_loop(0, 32, chunk, 0)

    def spread_rows(values, target):
        for i in range(4):
            target[128 * i : 128 * i + 128, :] = spread(values[i : i + 1, :])

    send_cols(0)
    loads[3].wait()
    for i in range(4):
        unit, norm = masked(student_v, i)
        rows = slice(128 * i, 128 * i + 128)
        s_send[rows, :] = unit
        s_cast[rows, :] = unit.astype(BF16)
        s_inv[rows, :] = jnp.broadcast_to(1.0 / norm, (128, 128))
        s_unit_t[:, rows] = jnp.transpose(unit)
    ts = [
        remote(t_send, t_other, ts_ssem.at[0], ts_rsem.at[0], partner),
        remote(s_send, s_other, ts_ssem.at[1], ts_rsem.at[1], partner),
    ]
    take_cols(0)
    row_pass(r1buf)
    send_rows(r1buf, 0)
    for copy in ts:
        copy.start()

    half = core * 2048
    tot_acc[...] = jnp.zeros_like(tot_acc)
    fp[...] = jnp.zeros_like(fp)

    def student_cols(j, keep):
        at = lax.rem(j * W + half, 4096)
        cols = pl.ds(pl.multiple_of(at, W), W)
        block = jnp.exp2(dot(s_cast[...], pc[:, cols]) * student_scale)
        for q in range(W // 128):
            tot_acc[...] += block[:, 128 * q : 128 * q + 128]
        high, low = split(block)
        if keep:
            mine = pl.ds(pl.multiple_of(j * W, W), W)
            x2h[0:512, mine] = high
            x2l[0:512, mine] = low
        fp[...] += (
            dot_cols(high, pc[:, cols]) + dot_cols(low, pc[:, cols]) + dot_cols(high, plo[:, cols])
        )

    def student_mine(j, carry):
        student_cols(j, True)
        return carry

    def student_rest(j, carry):
        student_cols(j, False)
        return carry

    lax.fori_loop(0, 4, student_mine, 0)
    lax.fori_loop(4, 8, student_rest, 0)
    for i in range(4):
        r2buf[pr, 4 + i : 5 + i, :] = jnp.sum(
            jnp.transpose(tot_acc[128 * i : 128 * i + 128, :]), axis=0, keepdims=True
        )
    spread_rows(1.0 / take_rows(r1buf, 0), ub)
    col_pass(1)

    send_cols(1)
    for copy in ts:
        copy.wait_recv()
    t_cast[...] = t_other[...].astype(BF16)
    s_cast[...] = s_other[...].astype(BF16)

    def own_split(j, carry):
        cols = pl.ds(pl.multiple_of(j * W + half, W), W)
        mine = pl.ds(pl.multiple_of(j * W, W), W)
        high, low = split(expos[:, cols])
        e2h[0:512, mine] = high
        e2l[0:512, mine] = low
        return carry

    lax.fori_loop(0, 4, own_split, 0)
    for i in range(4):
        s_unit_t[:, 512 + 128 * i : 640 + 128 * i] = jnp.transpose(
            s_other[128 * i : 128 * i + 128, :]
        )
    take_cols(1)
    row_pass(r2buf)
    send_rows(r2buf, 1)

    def send_y(q, src):
        for dy in (2, 1, 3):
            ty = lax.rem(y + dy, NY)
            remote(
                src.at[pl.ds(pl.multiple_of(ty * 128, 128), 128)], yr.at[q, dy - 1],
                y_ssem.at[q], y_rsem.at[q], proto_peer(dy, 0),
            ).start()

    def take_y(q, src):
        wait_bytes(yr.at[q], y_rsem.at[q])
        own = pl.ds(pl.multiple_of(y * 128, 128), 128)
        ysum[q] = src[own, :] + yr[q, 0] + yr[q, 1] + yr[q, 2]

    def send_z(q):
        for dz in (4, 3, 5, 2, 6, 1, 7):
            tz = lax.rem(z + dz, NZ)
            remote(
                ysum.at[q, pl.ds(pl.multiple_of(tz * 16, 16), 16)], zr.at[q, dz - 1],
                z_ssem.at[q], z_rsem.at[q], proto_peer(0, dz),
            ).start()

    def take_z(q):
        wait_bytes(zr.at[q], z_rsem.at[q])
        total = ysum[q, pl.ds(pl.multiple_of(z * 16, 16), 16), :]
        for k in range(7):
            total += zr[q, k]
        return total

    def other_cols(j, carry):
        cols = pl.ds(pl.multiple_of(j * W + half, W), W)
        mine = pl.ds(pl.multiple_of(j * W, W), W)
        high, low = split(jnp.exp2(dot(t_cast[...], pc[:, cols]) * teacher_scale))
        e2h[512:1024, mine] = high
        e2l[512:1024, mine] = low
        high, low = split(jnp.exp2(dot(s_cast[...], pc[:, cols]) * student_scale))
        x2h[512:1024, mine] = high
        x2l[512:1024, mine] = low
        return carry

    lax.fori_loop(0, 4, other_cols, 0)
    sums = take_rows(r2buf, 1)
    spread_rows(1.0 / sums[0:4, :], ub)
    tot_row[...] = 1.0 / sums[4:8, :]
    col_pass(2)

    send_cols(2)
    swap_s[0] = tot_row[...]
    swap_tot = remote(swap_s.at[0], swap_r.at[0], swap_ssem.at[0], swap_rsem.at[0], partner)
    swap_tot.start()
    send_y(0, fp)
    spread_rows(tot_row[...], totb)
    swap_tot.wait_recv()

    def scale_rows(own_ref, other_ref):
        for i in range(4):
            cols = slice(128 * i, 128 * i + 128)
            high, low = split(s_unit_t[:, cols] * own_ref[i : i + 1, :])
            a_hi[:, cols] = high
            a_lo[:, cols] = low
            cols = slice(512 + 128 * i, 640 + 128 * i)
            high, low = split(s_unit_t[:, cols] * other_ref[i : i + 1, :])
            a_hi[:, cols] = high
            a_lo[:, cols] = low

    def weigh(high, low, cols):
        return (
            dot(a_hi[...], high[:, cols]) + dot(a_lo[...], high[:, cols]) + dot(a_hi[...], low[:, cols])
        )

    scale_rows(tot_row, swap_r.at[0])

    def probs_part(j, carry):
        mine = pl.ds(pl.multiple_of(j * W, W), W)
        wtp[:, mine] = weigh(x2h, x2l, mine)
        return carry

    lax.fori_loop(0, 4, probs_part, 0)
    take_cols(2)
    row_pass(r3buf)
    send_rows(r3buf, 2)

    ft[...] = jnp.zeros_like(ft)

    def target_cols(j, carry):
        cols = pl.ds(pl.multiple_of(j * W, W), W)
        unit = pc[:, cols].astype(F32) + plo[:, cols].astype(F32)
        scaled = jnp.concatenate(
            [
                unit[:, 128 * q : 128 * q + 128] * vrow[pl.ds(4 * j + q, 1), :]
                for q in range(W // 128)
            ],
            axis=1,
        )
        b_high, b_low = split(scaled)
        high, low = split(expos[:, cols])
        ft[...] += dot_cols(high, b_high) + dot_cols(low, b_high) + dot_cols(high, b_low)
        return carry

    lax.fori_loop(0, 8, target_cols, 0)
    take_y(0, fp)
    send_z(0)
    send_y(1, ft)
    swap_s[1] = 1.0 / take_rows(r3buf, 2)
    swap_u = remote(swap_s.at[1], swap_r.at[1], swap_ssem.at[1], swap_rsem.at[1], partner)
    swap_u.start()
    spread_rows(swap_s[1], ub)
    swap_u.wait_recv()
    scale_rows(swap_s.at[1], swap_r.at[1])

    def block(d, offset, size):
        return pl.ds(pl.multiple_of(d * 64 + offset, 32), size)

    def protos_part(j, carry):
        mine = pl.ds(pl.multiple_of(j * W, W), W)
        cols = pl.ds(pl.multiple_of(j * W + half, W), W)
        target = weigh(e2h, e2l, mine)
        at = half // 128 + 4 * j
        target = jnp.concatenate(
            [
                target[:, 128 * q : 128 * q + 128] * vrow[pl.ds(at + q, 1), :]
                for q in range(W // 128)
            ],
            axis=1,
        )
        total = wtp[:, mine] - target
        unit = pc[:, cols].astype(F32) + plo[:, cols].astype(F32)
        inner = jnp.sum(unit * total, axis=0, keepdims=True)
        gpart[j] = (total - unit * inner) * (pinv[:, cols] * slope_scale)
        remote(gpart.at[j, block(x_far, 0, 32)], p1r.at[j, 0], p1_ssem.at[j, 0], p1_rsem.at[j, 0], right).start()
        remote(gpart.at[j, block(x_far, 32, 32)], p1r.at[j, 1], p1_ssem.at[j, 1], p1_rsem.at[j, 1], left).start()
        return carry

    lax.fori_loop(0, 4, protos_part, 0)

    def pass_on(j, carry):
        wait_bytes(p1r.at[j, 0], p1_rsem.at[j, 0])
        gpart[j, block(x_next, 0, 32), :] += p1r[j, 0]
        remote(gpart.at[j, block(x_next, 0, 64)], p2r.at[j, 0], p2_ssem.at[j, 0], p2_rsem.at[j, 0], right).start()
        wait_bytes(p1r.at[j, 1], p1_rsem.at[j, 1])
        gpart[j, block(x_prev, 32, 32), :] += p1r[j, 1]
        remote(gpart.at[j, block(x_prev, 0, 64)], p2r.at[j, 1], p2_ssem.at[j, 1], p2_rsem.at[j, 1], left).start()
        return carry

    lax.fori_loop(0, 4, pass_on, 0)

    take_y(1, ft)
    send_z(1)
    own16 = pl.ds(pl.multiple_of(y * 128 + z * 16, 16), 16)
    by_probs = take_z(0)
    by_target = take_z(1)
    unit = s_send[own16, :]
    scale_p = jnp.concatenate([totb[own16, :]] * 2, axis=1)
    scale_t = jnp.concatenate([ub[own16, :]] * 2, axis=1)
    grad = slope_scale * (by_probs * scale_p - by_target * scale_t)
    inner = jnp.sum(unit * grad, axis=1, keepdims=True)
    ag[y, z] = (grad - unit * inner) * jnp.concatenate([s_inv[own16, :]] * 2, axis=1)
    for dz in (4, 3, 5, 2, 6, 1, 7):
        remote(ag.at[y, z], ag.at[y, z], agz_ssem, agz_rsem, proto_peer(0, dz)).start()

    def finish(j, carry):
        wait_bytes(p2r.at[j, 0], p2_rsem.at[j, 0])
        wait_bytes(p2r.at[j, 1], p2_rsem.at[j, 1])

        def rows_of(c):
            at = pl.multiple_of(c * 32, 32)
            return (
                gpart[j, block(x, at, 32), :] + p2r[j, 0, pl.ds(at, 32), :] + p2r[j, 1, pl.ds(at, 32), :]
            )

        fin_s[j] = rows_of(1 - core)
        remote(fin_s.at[j], fin_r.at[j], fin_ssem.at[j], fin_rsem.at[j], partner).start()
        gw_ref[:, pl.ds(pl.multiple_of(j * W + half, W), W)] = rows_of(core)
        return carry

    lax.fori_loop(0, 2, finish, 0)
    wait_bytes(ag.at[y, pl.ds(0, 7)], agz_rsem)
    for dy in (2, 1, 3):
        remote(ag.at[y], ag.at[y], agy_ssem, agy_rsem, proto_peer(dy, 0)).start()
    lax.fori_loop(2, 4, finish, 0)

    def finish_other(j, carry):
        wait_bytes(fin_r.at[j], fin_rsem.at[j])
        at = pl.multiple_of(j * W + 2048 - half, W)
        gw_ref[:, pl.ds(at, W)] = fin_r[j]
        return carry

    lax.fori_loop(0, 4, finish_other, 0)
    wait_bytes(ag.at[pl.ds(0, 3)], agy_rsem)
    for i in range(4):
        rows = ag[i].reshape(128, 256)
        high, low = split(rows)
        rest = (rows - high.astype(F32) - low.astype(F32)).astype(BF16)
        gp_ref[256 * i : 256 * i + 256, :] = (
            dot(onehot[i], high) + dot(onehot[i], low) + dot(onehot[i], rest)
        )

    for t in range(3):
        wait_bytes(cbuf.at[t, pl.ds(0, 7)], c_ssem.at[t])
        buf = (r1buf, r2buf, r3buf)[t]
        wait_bytes(buf.at[pl.ds(0, 31)], r_ssem.at[t])
    for copy in ts:
        copy.wait_send()
    swap_tot.wait_send()
    swap_u.wait_send()
    for q in range(2):
        wait_bytes(yr.at[q], y_ssem.at[q])
        wait_bytes(zr.at[q], z_ssem.at[q])
    wait_bytes(ag.at[0, pl.ds(0, 7)], agz_ssem)
    wait_bytes(ag.at[pl.ds(0, 3)], agy_ssem)

    def drain(j, carry):
        for s in range(2):
            wait_bytes(p1r.at[j, s], p1_ssem.at[j, s])
            wait_bytes(p2r.at[j, s], p2_ssem.at[j, s])
        wait_bytes(fin_s.at[j], fin_ssem.at[j])
        return carry

    lax.fori_loop(0, 4, drain, 0)


def body(student_patches, teacher_patches, masked_index, prototypes):
    dma = pltpu.SemaphoreType.DMA

    def vmem(*shape, dtype=F32):
        return pltpu.VMEM(shape, dtype)

    def half_vmem(*shape):
        return pltpu.VMEM(shape, BF16)

    scratch = [
        half_vmem(1024, 256), half_vmem(1024, 256), vmem(4, 128, dtype=jnp.int32), half_vmem(256, 4096), dma((4,)),
        half_vmem(4, 256, 128), vmem(512, 256), vmem(512, 256), vmem(512, 256), vmem(512, 256),
        half_vmem(512, 256), half_vmem(512, 256), vmem(256, 1024), vmem(512, 128),
        half_vmem(256, 4096), half_vmem(256, 4096), vmem(1, 4096), vmem(512, 4096),
        half_vmem(1024, 2048), half_vmem(1024, 2048), half_vmem(1024, 2048), half_vmem(1024, 2048),
        vmem(256, 2048), half_vmem(256, 1024), half_vmem(256, 1024),
        vmem(3, 8, 32, 128), dma((3,)), dma((3,)),
        vmem(32, 4, 128), vmem(32, 8, 128), vmem(32, 4, 128), dma((3,)), dma((3,)),
        vmem(512, 128), vmem(32, 128), vmem(4, 128), vmem(512, 128), vmem(512, 128),
        dma((2,)), dma((2,)), vmem(2, 4, 128), vmem(2, 4, 128), dma((2,)), dma((2,)),
        vmem(512, 256), vmem(512, 256), vmem(2, 3, 128, 256), vmem(2, 128, 256), dma((2,)), dma((2,)),
        vmem(2, 7, 16, 256), dma((2,)), dma((2,)),
        vmem(4, 8, 16, 256), dma, dma, dma, dma,
        vmem(4, 256, 512), vmem(4, 2, 32, 512), dma((4, 2)), dma((4, 2)),
        vmem(4, 2, 64, 512), dma((4, 2)), dma((4, 2)),
        vmem(4, 32, 512), vmem(4, 32, 512), dma((4,)), dma((4,)),
    ]
    return pl.pallas_call(
        kernel,
        out_shape=(
            jax.ShapeDtypeStruct((1024, 256), F32),
            jax.ShapeDtypeStruct((32, 4096), F32),
        ),
        in_specs=[pl.BlockSpec(memory_space=pl.ANY)] * 4,
        out_specs=(pl.BlockSpec(memory_space=pltpu.VMEM), pl.BlockSpec(memory_space=pltpu.VMEM)),
        scratch_shapes=scratch,
        compiler_params=pltpu.CompilerParams(
            collective_id=0, has_side_effects=True, vmem_limit_bytes=60 * 1024 * 1024
        ),
    )(student_patches, teacher_patches, masked_index, prototypes)


def solution(mesh):
    placed = (P("dp", None), P("dp", None), P("dp", None), P(None, "proto"))
    return jax.shard_map(
        body,
        mesh=mesh,
        in_specs=placed,
        out_specs=(P("dp", None), P("dp", "proto")),
        check_vma=False,
    )
```

time: 587 us -> 84.1 us (0.14)
  the two profiles are of different devices: /device:TPU:1 before, /device:TPU:8 now
where the time goes in v1:
time: 84.1 us; the launch traced here: 83.9 us
  Pallas kernels  80.2 us (95%)
  local copies, waits for them, and re-layouts  3.12 us (4%)
    pallas_call x1, Pallas kernels, body(): pl.pallas_call(kernel, out_shape=(jax.ShapeDtypeStruct((1024, 256), F32),...  80.2 us
    unnamed x4, local copies, waits for them, and re-layouts  3.12 us

profile of v1, /device:TPU:8, one launch (start us, length us, event | category | flops | bytes accessed | tf_op | source)
XLA Modules:
  0.0 83.9 jit_solution(14001766202095799436)
XLA Ops:
  0.6 80.2 %shard_map.59 = (f32[1024,256]{1,0:T(8,128)}, f32[32,4096]{1,0:T(8,128)}) custom-call(bf16[1024,256]{1,0:T(8,128)(2,1)} %student_hbm.1, bf16[1024,256]{1,0:T(8,128)(2,1)} %teacher_hbm.1, s32[4,128]{1,0:T(4,128)} %index_hbm.1, bf16[256,4096]{1,0:T(8,128)(2,1)} %protos_hbm.1), custom_call_target="tpu_custom_call" | custom-call | tf_op jit(solution)/shard_map/pallas_call | solution.py:504
  80.8 0.0 copy-start
  80.8 2.3 %copy.8 = f32[1024,256]{1,0:T(8,128)} copy(f32[1024,256]{1,0:T(8,128)} %get-tuple-element.4) | data formatting | bytes 2097152
  83.1 0.0 copy-done
  83.1 0.8 copy.9
Async XLA Ops:
  80.8 2.3 %copy-start = (f32[32,4096]{1,0:T(8,128)S(1)}, f32[32,4096]{1,0:T(8,128)}, u32[]{:S(2)}) copy-start(f32[32,4096]{1,0:T(8,128)} %get-tuple-element.5) | copy-start | bytes 1572868

commit v2 on v1

--- a/solution.py
+++ b/solution.py
@@ -17,6 +17,7 @@
 epsilon = 1e-06
 
 W = 512
+V = 256
 NY, NZ = 4, 8
 FAR_FIRST = sorted(
     [(dy, dz) for dy in range(NY) for dz in range(NZ) if dy or dz],
@@ -39,18 +40,18 @@
 
 def kernel(
     student_hbm, teacher_hbm, index_hbm, protos_hbm,
-    gp_ref, gw_ref,
+    rows_hbm, gw_hbm,
     student_v, teacher_v, index_v, protos_v, in_sem,
     onehot, t_send, s_send, t_other, s_other, t_cast, s_cast, s_unit_t, s_inv,
     pc, plo, pinv, expos,
     e2h, e2l, x2h, x2l, wtp, a_hi, a_lo,
     cbuf, c_ssem, c_rsem,
-    r1buf, r2buf, r3buf, r_ssem, r_rsem, ub, vrow, tot_row, tot_acc, totb,
+    r1buf, r2buf, r3buf, tbuf, r_ssem, r_rsem, ub, vrow, tot_row, tot_acc, totb,
     ts_ssem, ts_rsem, swap_s, swap_r, swap_ssem, swap_rsem,
     fp, ft, yr, ysum, y_ssem, y_rsem, zr, z_ssem, z_rsem,
     ag, agz_ssem, agz_rsem, agy_ssem, agy_rsem,
     gpart, p1r, p1_ssem, p1_rsem, p2r, p2_ssem, p2_rsem,
-    fin_s, fin_r, fin_ssem, fin_rsem,
+    fin_s, fin_r, fin_ssem, fin_rsem, gw_ref, out_sem,
 ):
     dp = lax.axis_index("dp")
     pr = lax.axis_index("proto")
@@ -75,6 +76,16 @@
     def wait_bytes(ref, sem):
         pltpu.make_async_copy(ref, ref, sem).wait()
 
+    def load(src, dst, sem, parts):
+        size = src.shape[0] // parts
+        for i in range(parts):
+            rows = pl.ds(i * size, size)
+            pltpu.make_async_copy(src.at[rows], dst.at[rows], sem).start()
+
+    load(index_hbm, index_v, in_sem.at[0], 1)
+    load(teacher_hbm, teacher_v, in_sem.at[1], 4)
+    load(protos_hbm, protos_v, in_sem.at[2], 8)
+    load(student_hbm, student_v, in_sem.at[3], 4)
     barrier = pltpu.get_barrier_semaphore()
     for k in range(1, 8):
         pl.semaphore_signal(barrier, inc=1, device_id=dp_peer(k), device_id_type=MESH)
@@ -82,16 +93,8 @@
         pl.semaphore_signal(
             barrier, inc=1, device_id=proto_peer(dy, dz), device_id_type=MESH
         )
-    loads = [
-        pltpu.make_async_copy(src, dst, in_sem.at[i])
-        for i, (src, dst) in enumerate(
-            [(index_hbm, index_v), (teacher_hbm, teacher_v), (protos_hbm, protos_v), (student_hbm, student_v)]
-        )
-    ]
-    for load in loads:
-        load.start()
-
-    loads[0].wait()
+
+    wait_bytes(index_v, in_sem.at[0])
     for i in range(4):
         places = lax.broadcasted_iota(jnp.int32, (256, 128), 0)
         onehot[i] = jnp.where(places == index_v[i : i + 1, :], 1.0, 0.0).astype(BF16)
@@ -104,7 +107,7 @@
         norm = jnp.sqrt(jnp.sum(rows * rows, axis=1, keepdims=True) + epsilon)
         return rows / norm, norm
 
-    loads[1].wait()
+    wait_bytes(teacher_v, in_sem.at[1])
     for i in range(4):
         unit, _ = masked(teacher_v, i)
         t_send[128 * i : 128 * i + 128, :] = unit
@@ -114,7 +117,7 @@
         for q in range(W // 128):
             buf[slot, pl.ds(4 * j + q, 1), :] = sums[:, 128 * q : 128 * q + 128]
 
-    loads[2].wait()
+    wait_bytes(protos_v, in_sem.at[2])
 
     def front(j, carry):
         cols = pl.ds(pl.multiple_of(j * W, W), W)
@@ -129,7 +132,7 @@
         put_cols(cbuf.at[0], dp, j, jnp.sum(block, axis=0, keepdims=True))
         return carry
 
-    lax.fori_loop(0, 8, front, 0)
+    lax.fori_loop(0, 8, front, 0, unroll=2)
     pl.semaphore_wait(barrier, 7 + len(FAR_FIRST))
 
     def send_cols(t):
@@ -152,32 +155,33 @@
         return jnp.transpose(jnp.broadcast_to(row, (128, 128)))
 
     def row_pass(buf):
-        def image(i, carry):
-            rows = pl.ds(pl.multiple_of(i * 128, 128), 128)
+        for i in range(4):
+            rows = slice(128 * i, 128 * i + 128)
             total = expos[rows, 0:128] * vrow[0:1, :]
             for k in range(1, 32):
                 total += expos[rows, 128 * k : 128 * k + 128] * vrow[k : k + 1, :]
-            buf[pr, pl.ds(i, 1), :] = jnp.sum(jnp.transpose(total), axis=0, keepdims=True)
+            buf[pr, i : i + 1, :] = jnp.sum(jnp.transpose(total), axis=0, keepdims=True)
+
+    def col_pass(t):
+        def chunk(j, carry):
+            cols = pl.ds(pl.multiple_of(j * 1024, 1024), 1024)
+            sums = jnp.zeros((8, 1024), F32)
+            for i in range(64):
+                scale = ub[8 * i : 8 * i + 8, :]
+                sums += expos[8 * i : 8 * i + 8, cols] * jnp.concatenate([scale] * 8, axis=1)
+            total = jnp.sum(sums, axis=0, keepdims=True)
+            for q in range(8):
+                cbuf[t, dp, pl.ds(8 * j + q, 1), :] = total[:, 128 * q : 128 * q + 128]
             return carry
 
-        lax.fori_loop(0, 4, image, 0)
-
-    def col_pass(t):
-        def chunk(k, carry):
-            cols = pl.ds(pl.multiple_of(k * 128, 128), 128)
-            cbuf[t, dp, pl.ds(k, 1), :] = jnp.sum(
-                expos[:, cols] * ub[...], axis=0, keepdims=True
-            )
-            return carry
-
-        lax.fori_loop(0, 32, chunk, 0)
+        lax.fori_loop(0, 4, chunk, 0)
 
     def spread_rows(values, target):
         for i in range(4):
             target[128 * i : 128 * i + 128, :] = spread(values[i : i + 1, :])
 
     send_cols(0)
-    loads[3].wait()
+    wait_bytes(student_v, in_sem.at[3])
     for i in range(4):
         unit, norm = masked(student_v, i)
         rows = slice(128 * i, 128 * i + 128)
@@ -189,9 +193,6 @@
         remote(t_send, t_other, ts_ssem.at[0], ts_rsem.at[0], partner),
         remote(s_send, s_other, ts_ssem.at[1], ts_rsem.at[1], partner),
     ]
-    take_cols(0)
-    row_pass(r1buf)
-    send_rows(r1buf, 0)
     for copy in ts:
         copy.start()
 
@@ -223,64 +224,20 @@
         return carry
 
     lax.fori_loop(0, 4, student_mine, 0)
+    take_cols(0)
+    row_pass(r1buf)
+    send_rows(r1buf, 0)
+
     lax.fori_loop(4, 8, student_rest, 0)
     for i in range(4):
-        r2buf[pr, 4 + i : 5 + i, :] = jnp.sum(
+        tbuf[pr, i : i + 1, :] = jnp.sum(
             jnp.transpose(tot_acc[128 * i : 128 * i + 128, :]), axis=0, keepdims=True
         )
-    spread_rows(1.0 / take_rows(r1buf, 0), ub)
-    col_pass(1)
-
-    send_cols(1)
+    send_rows(tbuf, 3)
     for copy in ts:
         copy.wait_recv()
     t_cast[...] = t_other[...].astype(BF16)
     s_cast[...] = s_other[...].astype(BF16)
-
-    def own_split(j, carry):
-        cols = pl.ds(pl.multiple_of(j * W + half, W), W)
-        mine = pl.ds(pl.multiple_of(j * W, W), W)
-        high, low = split(expos[:, cols])
-        e2h[0:512, mine] = high
-        e2l[0:512, mine] = low
-        return carry
-
-    lax.fori_loop(0, 4, own_split, 0)
-    for i in range(4):
-        s_unit_t[:, 512 + 128 * i : 640 + 128 * i] = jnp.transpose(
-            s_other[128 * i : 128 * i + 128, :]
-        )
-    take_cols(1)
-    row_pass(r2buf)
-    send_rows(r2buf, 1)
-
-    def send_y(q, src):
-        for dy in (2, 1, 3):
-            ty = lax.rem(y + dy, NY)
-            remote(
-                src.at[pl.ds(pl.multiple_of(ty * 128, 128), 128)], yr.at[q, dy - 1],
-                y_ssem.at[q], y_rsem.at[q], proto_peer(dy, 0),
-            ).start()
-
-    def take_y(q, src):
-        wait_bytes(yr.at[q], y_rsem.at[q])
-        own = pl.ds(pl.multiple_of(y * 128, 128), 128)
-        ysum[q] = src[own, :] + yr[q, 0] + yr[q, 1] + yr[q, 2]
-
-    def send_z(q):
-        for dz in (4, 3, 5, 2, 6, 1, 7):
-            tz = lax.rem(z + dz, NZ)
-            remote(
-                ysum.at[q, pl.ds(pl.multiple_of(tz * 16, 16), 16)], zr.at[q, dz - 1],
-                z_ssem.at[q], z_rsem.at[q], proto_peer(0, dz),
-            ).start()
-
-    def take_z(q):
-        wait_bytes(zr.at[q], z_rsem.at[q])
-        total = ysum[q, pl.ds(pl.multiple_of(z * 16, 16), 16), :]
-        for k in range(7):
-            total += zr[q, k]
-        return total
 
     def other_cols(j, carry):
         cols = pl.ds(pl.multiple_of(j * W + half, W), W)
@@ -294,36 +251,76 @@
         return carry
 
     lax.fori_loop(0, 4, other_cols, 0)
-    sums = take_rows(r2buf, 1)
-    spread_rows(1.0 / sums[0:4, :], ub)
-    tot_row[...] = 1.0 / sums[4:8, :]
-    col_pass(2)
-
-    send_cols(2)
+    spread_rows(1.0 / take_rows(r1buf, 0), ub)
+    col_pass(1)
+
+    def send_y(q, src, steps):
+        for dy in steps:
+            ty = lax.rem(y + dy, NY)
+            remote(
+                src.at[pl.ds(pl.multiple_of(ty * 128, 128), 128)], yr.at[q, dy - 1],
+                y_ssem.at[q], y_rsem.at[q], proto_peer(dy, 0),
+            ).start()
+
+    def take_y(q, src):
+        wait_bytes(yr.at[q], y_rsem.at[q])
+        own = pl.ds(pl.multiple_of(y * 128, 128), 128)
+        ysum[q] = src[own, :] + yr[q, 0] + yr[q, 1] + yr[q, 2]
+
+    def send_z(q):
+        for dz in (4, 3, 5, 2, 6, 1, 7):
+            tz = lax.rem(z + dz, NZ)
+            remote(
+                ysum.at[q, pl.ds(pl.multiple_of(tz * 16, 16), 16)], zr.at[q, dz - 1],
+                z_ssem.at[q], z_rsem.at[q], proto_peer(0, dz),
+            ).start()
+
+    def take_z(q):
+        wait_bytes(zr.at[q], z_rsem.at[q])
+        total = ysum[q, pl.ds(pl.multiple_of(z * 16, 16), 16), :]
+        for k in range(7):
+            total += zr[q, k]
+        return total
+
+    send_cols(1)
+    send_y(0, fp, (2,))
+    take_cols(1)
+    row_pass(r2buf)
+    send_rows(r2buf, 1)
+
+    def scale_half(at, ref):
+        for i in range(4):
+            cols = slice(at + 128 * i, at + 128 * i + 128)
+            high, low = split(s_unit_t[:, cols] * ref[i : i + 1, :])
+            a_hi[:, cols] = high
+            a_lo[:, cols] = low
+
+    def weigh(high, low, cols):
+        return (
+            dot(a_hi[...], high[:, cols]) + dot(a_lo[...], high[:, cols]) + dot(a_hi[...], low[:, cols])
+        )
+
+    tot_row[...] = 1.0 / take_rows(tbuf, 3)
     swap_s[0] = tot_row[...]
     swap_tot = remote(swap_s.at[0], swap_r.at[0], swap_ssem.at[0], swap_rsem.at[0], partner)
     swap_tot.start()
-    send_y(0, fp)
     spread_rows(tot_row[...], totb)
+    def own_split(j, carry):
+        cols = pl.ds(pl.multiple_of(j * W + half, W), W)
+        mine = pl.ds(pl.multiple_of(j * W, W), W)
+        high, low = split(expos[:, cols])
+        e2h[0:512, mine] = high
+        e2l[0:512, mine] = low
+        return carry
+
+    lax.fori_loop(0, 4, own_split, 0)
+    for i in range(4):
+        s_unit_t[:, 512 + 128 * i : 640 + 128 * i] = jnp.transpose(
+            s_other[128 * i : 128 * i + 128, :]
+        )
+    scale_half(0, tot_row)
     swap_tot.wait_recv()
-
-    def scale_rows(own_ref, other_ref):
-        for i in range(4):
-            cols = slice(128 * i, 128 * i + 128)
-            high, low = split(s_unit_t[:, cols] * own_ref[i : i + 1, :])
-            a_hi[:, cols] = high
-            a_lo[:, cols] = low
-            cols = slice(512 + 128 * i, 640 + 128 * i)
-            high, low = split(s_unit_t[:, cols] * other_ref[i : i + 1, :])
-            a_hi[:, cols] = high
-            a_lo[:, cols] = low
-
-    def weigh(high, low, cols):
-        return (
-            dot(a_hi[...], high[:, cols]) + dot(a_lo[...], high[:, cols]) + dot(a_hi[...], low[:, cols])
-        )
-
-    scale_rows(tot_row, swap_r.at[0])
+    scale_half(512, swap_r.at[0])
 
     def probs_part(j, carry):
         mine = pl.ds(pl.multiple_of(j * W, W), W)
@@ -331,6 +328,11 @@
         return carry
 
     lax.fori_loop(0, 4, probs_part, 0)
+    spread_rows(1.0 / take_rows(r2buf, 1), ub)
+    col_pass(2)
+
+    send_cols(2)
+    send_y(0, fp, (1, 3))
     take_cols(2)
     row_pass(r3buf)
     send_rows(r3buf, 2)
@@ -355,26 +357,21 @@
     lax.fori_loop(0, 8, target_cols, 0)
     take_y(0, fp)
     send_z(0)
-    send_y(1, ft)
+    send_y(1, ft, (2, 1, 3))
     swap_s[1] = 1.0 / take_rows(r3buf, 2)
     swap_u = remote(swap_s.at[1], swap_r.at[1], swap_ssem.at[1], swap_rsem.at[1], partner)
     swap_u.start()
-    spread_rows(swap_s[1], ub)
-    swap_u.wait_recv()
-    scale_rows(swap_s.at[1], swap_r.at[1])
-
     def block(d, offset, size):
         return pl.ds(pl.multiple_of(d * 64 + offset, 32), size)
 
-    def protos_part(j, carry):
-        mine = pl.ds(pl.multiple_of(j * W, W), W)
-        cols = pl.ds(pl.multiple_of(j * W + half, W), W)
-        target = weigh(e2h, e2l, mine)
-        at = half // 128 + 4 * j
+    def protos_part(j, target):
+        mine = pl.ds(pl.multiple_of(j * V, V), V)
+        cols = pl.ds(pl.multiple_of(j * V + half, V), V)
+        at = half // 128 + V // 128 * j
         target = jnp.concatenate(
             [
                 target[:, 128 * q : 128 * q + 128] * vrow[pl.ds(at + q, 1), :]
-                for q in range(W // 128)
+                for q in range(V // 128)
             ],
             axis=1,
         )
@@ -384,9 +381,26 @@
         gpart[j] = (total - unit * inner) * (pinv[:, cols] * slope_scale)
         remote(gpart.at[j, block(x_far, 0, 32)], p1r.at[j, 0], p1_ssem.at[j, 0], p1_rsem.at[j, 0], right).start()
         remote(gpart.at[j, block(x_far, 32, 32)], p1r.at[j, 1], p1_ssem.at[j, 1], p1_rsem.at[j, 1], left).start()
-        return carry
-
-    lax.fori_loop(0, 4, protos_part, 0)
+
+    def weigh_some(rows, cols):
+        return (
+            dot(a_hi[:, rows], e2h[rows, cols])
+            + dot(a_lo[:, rows], e2h[rows, cols])
+            + dot(a_hi[:, rows], e2l[rows, cols])
+        )
+
+    first = pl.ds(0, V)
+    scale_half(0, swap_s.at[1])
+    target = weigh_some(slice(0, 512), first)
+    swap_u.wait_recv()
+    scale_half(512, swap_r.at[1])
+    protos_part(0, target + weigh_some(slice(512, 1024), first))
+
+    def protos_rest(j, carry):
+        protos_part(j, weigh(e2h, e2l, pl.ds(pl.multiple_of(j * V, V), V)))
+        return carry
+
+    lax.fori_loop(1, 8, protos_rest, 0)
 
     def pass_on(j, carry):
         wait_bytes(p1r.at[j, 0], p1_rsem.at[j, 0])
@@ -397,10 +411,12 @@
         remote(gpart.at[j, block(x_prev, 0, 64)], p2r.at[j, 1], p2_ssem.at[j, 1], p2_rsem.at[j, 1], left).start()
         return carry
 
-    lax.fori_loop(0, 4, pass_on, 0)
-
+    lax.fori_loop(0, 3, pass_on, 0)
     take_y(1, ft)
     send_z(1)
+    lax.fori_loop(3, 8, pass_on, 0)
+    spread_rows(swap_s[1], ub)
+
     own16 = pl.ds(pl.multiple_of(y * 128 + z * 16, 16), 16)
     by_probs = take_z(0)
     by_target = take_z(1)
@@ -411,7 +427,13 @@
     inner = jnp.sum(unit * grad, axis=1, keepdims=True)
     ag[y, z] = (grad - unit * inner) * jnp.concatenate([s_inv[own16, :]] * 2, axis=1)
     for dz in (4, 3, 5, 2, 6, 1, 7):
-        remote(ag.at[y, z], ag.at[y, z], agz_ssem, agz_rsem, proto_peer(0, dz)).start()
+        remote(ag.at[y, z], ag.at[y, z], agz_ssem.at[dz - 1], agz_rsem.at[dz - 1], proto_peer(0, dz)).start()
+
+    def to_y(piece):
+        for dy in (2, 1, 3):
+            remote(piece, piece, agy_ssem, agy_rsem, proto_peer(dy, 0)).start()
+
+    to_y(ag.at[y, z])
 
     def finish(j, carry):
         wait_bytes(p2r.at[j, 0], p2_rsem.at[j, 0])
@@ -425,34 +447,32 @@
 
         fin_s[j] = rows_of(1 - core)
         remote(fin_s.at[j], fin_r.at[j], fin_ssem.at[j], fin_rsem.at[j], partner).start()
-        gw_ref[:, pl.ds(pl.multiple_of(j * W + half, W), W)] = rows_of(core)
+        gw_ref[j] = rows_of(core)
+        at = pl.multiple_of(j * V + half, V)
+        pltpu.make_async_copy(gw_ref.at[j], gw_hbm.at[:, pl.ds(at, V)], out_sem.at[0]).start()
         return carry
 
     lax.fori_loop(0, 2, finish, 0)
-    wait_bytes(ag.at[y, pl.ds(0, 7)], agz_rsem)
-    for dy in (2, 1, 3):
-        remote(ag.at[y], ag.at[y], agy_ssem, agy_rsem, proto_peer(dy, 0)).start()
-    lax.fori_loop(2, 4, finish, 0)
+    for dz in (1, 7, 2, 6, 3, 5, 4):
+        piece = ag.at[y, lax.rem(z + NZ - dz, NZ)]
+        wait_bytes(piece, agz_rsem.at[dz - 1])
+        to_y(piece)
+    lax.fori_loop(2, 8, finish, 0)
 
     def finish_other(j, carry):
         wait_bytes(fin_r.at[j], fin_rsem.at[j])
-        at = pl.multiple_of(j * W + 2048 - half, W)
-        gw_ref[:, pl.ds(at, W)] = fin_r[j]
-        return carry
-
-    lax.fori_loop(0, 4, finish_other, 0)
+        at = pl.multiple_of(j * V + 2048 - half, V)
+        pltpu.make_async_copy(fin_r.at[j], gw_hbm.at[:, pl.ds(at, V)], out_sem.at[0]).start()
+        return carry
+
+    lax.fori_loop(0, 8, finish_other, 0)
     wait_bytes(ag.at[pl.ds(0, 3)], agy_rsem)
-    for i in range(4):
-        rows = ag[i].reshape(128, 256)
-        high, low = split(rows)
-        rest = (rows - high.astype(F32) - low.astype(F32)).astype(BF16)
-        gp_ref[256 * i : 256 * i + 256, :] = (
-            dot(onehot[i], high) + dot(onehot[i], low) + dot(onehot[i], rest)
-        )
+    rows_out = pltpu.make_async_copy(ag, rows_hbm, out_sem.at[1])
+    rows_out.start()
 
     for t in range(3):
         wait_bytes(cbuf.at[t, pl.ds(0, 7)], c_ssem.at[t])
-        buf = (r1buf, r2buf, r3buf)[t]
+    for t, buf in enumerate((r1buf, r2buf, r3buf, tbuf)):
         wait_bytes(buf.at[pl.ds(0, 31)], r_ssem.at[t])
     for copy in ts:
         copy.wait_send()
@@ -461,7 +481,8 @@
     for q in range(2):
         wait_bytes(yr.at[q], y_ssem.at[q])
         wait_bytes(zr.at[q], z_ssem.at[q])
-    wait_bytes(ag.at[0, pl.ds(0, 7)], agz_ssem)
+    for k in range(7):
+        wait_bytes(ag.at[0, 0], agz_ssem.at[k])
     wait_bytes(ag.at[pl.ds(0, 3)], agy_ssem)
 
     def drain(j, carry):
@@ -471,7 +492,36 @@
         wait_bytes(fin_s.at[j], fin_ssem.at[j])
         return carry
 
-    lax.fori_loop(0, 4, drain, 0)
+    lax.fori_loop(0, 8, drain, 0)
+    wait_bytes(gw_ref, out_sem.at[0])
+    wait_bytes(fin_r, out_sem.at[0])
+    rows_out.wait()
+
+
+def place_kernel(rows_hbm, index_ref, gw_in, gp_hbm, gw_hbm, rows, placed, gw, sem, out_sem):
+    loads = [pltpu.make_async_copy(rows_hbm.at[i], rows.at[i], sem.at[i]) for i in range(4)]
+    gw_load = pltpu.make_async_copy(gw_in, gw, sem.at[4])
+    for copy in [*loads, gw_load]:
+        copy.start()
+    stores = []
+    for i in range(4):
+        places = lax.broadcasted_iota(jnp.int32, (256, 128), 0)
+        onehot = jnp.where(places == index_ref[i : i + 1, :], 1.0, 0.0).astype(BF16)
+        loads[i].wait()
+        value = rows[i]
+        high, low = split(value)
+        rest = (value - high.astype(F32) - low.astype(F32)).astype(BF16)
+        placed[i] = dot(onehot, high) + dot(onehot, low) + dot(onehot, rest)
+        stores.append(
+            pltpu.make_async_copy(placed.at[i], gp_hbm.at[pl.ds(256 * i, 256)], out_sem.at[i])
+        )
+        stores[-1].start()
+        if i == 1:
+            gw_load.wait()
+            stores.append(pltpu.make_async_copy(gw, gw_hbm, out_sem.at[4]))
+            stores[-1].start()
+    for copy in stores:
+        copy.wait()
 
 
 def body(student_patches, teacher_patches, masked_index, prototypes):
@@ -491,29 +541,40 @@
         half_vmem(1024, 2048), half_vmem(1024, 2048), half_vmem(1024, 2048), half_vmem(1024, 2048),
         vmem(256, 2048), half_vmem(256, 1024), half_vmem(256, 1024),
         vmem(3, 8, 32, 128), dma((3,)), dma((3,)),
-        vmem(32, 4, 128), vmem(32, 8, 128), vmem(32, 4, 128), dma((3,)), dma((3,)),
+        vmem(32, 4, 128), vmem(32, 4, 128), vmem(32, 4, 128), vmem(32, 4, 128), dma((4,)), dma((4,)),
         vmem(512, 128), vmem(32, 128), vmem(4, 128), vmem(512, 128), vmem(512, 128),
         dma((2,)), dma((2,)), vmem(2, 4, 128), vmem(2, 4, 128), dma((2,)), dma((2,)),
         vmem(512, 256), vmem(512, 256), vmem(2, 3, 128, 256), vmem(2, 128, 256), dma((2,)), dma((2,)),
         vmem(2, 7, 16, 256), dma((2,)), dma((2,)),
-        vmem(4, 8, 16, 256), dma, dma, dma, dma,
-        vmem(4, 256, 512), vmem(4, 2, 32, 512), dma((4, 2)), dma((4, 2)),
-        vmem(4, 2, 64, 512), dma((4, 2)), dma((4, 2)),
-        vmem(4, 32, 512), vmem(4, 32, 512), dma((4,)), dma((4,)),
+        vmem(4, 8, 16, 256), dma((7,)), dma((7,)), dma, dma,
+        vmem(8, 256, 256), vmem(8, 2, 32, 256), dma((8, 2)), dma((8, 2)),
+        vmem(8, 2, 64, 256), dma((8, 2)), dma((8, 2)),
+        vmem(8, 32, 256), vmem(8, 32, 256), dma((8,)), dma((8,)), vmem(8, 32, 256), dma((2,)),
     ]
-    return pl.pallas_call(
+    anywhere = pl.BlockSpec(memory_space=pl.ANY)
+    rows, grad_prototypes = pl.pallas_call(
         kernel,
         out_shape=(
-            jax.ShapeDtypeStruct((1024, 256), F32),
+            jax.ShapeDtypeStruct((4, 8, 16, 256), F32),
             jax.ShapeDtypeStruct((32, 4096), F32),
         ),
-        in_specs=[pl.BlockSpec(memory_space=pl.ANY)] * 4,
-        out_specs=(pl.BlockSpec(memory_space=pltpu.VMEM), pl.BlockSpec(memory_space=pltpu.VMEM)),
+        in_specs=[anywhere] * 4,
+        out_specs=(anywhere, anywhere),
         scratch_shapes=scratch,
         compiler_params=pltpu.CompilerParams(
             collective_id=0, has_side_effects=True, vmem_limit_bytes=60 * 1024 * 1024
         ),
     )(student_patches, teacher_patches, masked_index, prototypes)
+    return pl.pallas_call(
+        place_kernel,
+        out_shape=(
+            jax.ShapeDtypeStruct((1024, 256), F32),
+            jax.ShapeDtypeStruct((32, 4096), F32),
+        ),
+        in_specs=[anywhere, pl.BlockSpec(memory_space=pltpu.VMEM), anywhere],
+        out_specs=(anywhere, anywhere),
+        scratch_shapes=[vmem(4, 128, 256), vmem(4, 256, 256), vmem(32, 4096), dma((5,)), dma((5,))],
+    )(rows.reshape(4, 128, 256), masked_index, grad_prototypes)
 
 
 def solution(mesh):

time: 84.1 us -> 73.8 us (0.88)
  the two profiles are of different devices: /device:TPU:8 before, /device:TPU:1 now
where the time goes in v2:
time: 73.8 us; the launch traced here: 73.7 us
  Pallas kernels  73 us (99%)
    pallas_call x1, Pallas kernels, body(): pl.pallas_call(kernel, out_shape=(jax.ShapeDtypeStruct((4, 8, 16, 256), F...  69.3 us
    pallas_call x1, Pallas kernels, body(): pl.pallas_call(place_kernel, out_shape=(jax.ShapeDtypeStruct((1024, 256),...  3.78 us

profile of v2, /device:TPU:1, one launch (start us, length us, event | category | flops | bytes accessed | tf_op | source)
XLA Modules:
  0.0 73.7 jit_solution(2999986330051929070)
XLA Ops:
  0.6 69.3 %shard_map.59 = (f32[4,8,16,256]{3,2,1,0:T(8,128)}, f32[32,4096]{1,0:T(8,128)}) custom-call(bf16[1024,256]{1,0:T(8,128)(2,1)} %student_hbm.1, bf16[1024,256]{1,0:T(8,128)(2,1)} %teacher_hbm.1, s32[4,128]{1,0:T(4,128)} %index_ref.1, bf16[256,4096]{1,0:T(8,128)(2,1)} %protos_hbm.1), custom_call_target="tpu_custom_call" | custom-call | tf_op jit(solution)/shard_map/pallas_call | solution.py:555
  69.9 3.8 %shard_map.60 = (f32[1024,256]{1,0:T(8,128)}, f32[32,4096]{1,0:T(8,128)}) custom-call(f32[4,128,256]{2,1,0:T(8,128)} %bitcast.1, s32[4,128]{1,0:T(4,128)} %index_ref.1, f32[32,4096]{1,0:T(8,128)} %get-tuple-element.5.gw_in), custom_call_target="tpu_custom_call" | custom-call | tf_op jit(solution)/shard_map/pallas_call | solution.py:568

commit v3 on v2

v3 whole, which is shorter than its diff:
```python
import math

import jax
import jax.numpy as jnp
from jax import lax
from jax.experimental import pallas as pl
from jax.experimental.pallas import tpu as pltpu
from jax.sharding import PartitionSpec as P

MESH = pl.DeviceIdType.MESH
F32 = jnp.float32
BF16 = jnp.bfloat16

teacher_scale = math.log2(math.e) / 0.07
student_scale = math.log2(math.e) / 0.1
slope_scale = 4096.0 / 0.1
epsilon = 1e-06

W = 512
V = 256
NY, NZ = 4, 8
Z_FAR_FIRST = (4, 3, 5, 2, 6, 1, 7, 0)
FAR_FIRST = sorted(
    [(dy, dz) for dy in range(NY) for dz in range(NZ) if dy or dz],
    key=lambda o: -(min(o[0], NY - o[0]) + min(o[1], NZ - o[1])),
)


def dot(a, b):
    return jnp.dot(a, b, preferred_element_type=F32)


def dot_cols(a, b):
    return lax.dot_general(a, b, (((1,), (1,)), ((), ())), preferred_element_type=F32)


def split(value):
    high = value.astype(BF16)
    return high, (value - high.astype(F32)).astype(BF16)


def kernel(
    student_hbm, teacher_hbm, index_hbm, protos_hbm,
    rows_hbm, gw_hbm,
    student_v, teacher_v, index_v, protos_v, in_sem, protos_sem,
    onehot, t_send, s_send, t_other, s_other, t_cast, s_cast, s_unit_t, s_inv,
    pc, plo, pinv, expos,
    e2h, e2l, x2h, x2l, wtp, a_hi, a_lo,
    cbuf, c_ssem, c_rsem,
    rbuf, r_ssem, r_rsem, ub, row_acc, vrow, tot_row, tot_acc, totb,
    ts_ssem, ts_rsem, swap_s, swap_r, swap_ssem, swap_rsem,
    fp, ft, yr, ysum, y_ssem, y_rsem, yp_ssem, yp_rsem, zr, z_ssem, z_rsem,
    ag, agz_ssem, agz_rsem, agy_ssem, agy_rsem,
    gpart, p1r, p1_ssem, p1_rsem, p2r, p2_ssem, p2_rsem,
    gw_ref, out_sem,
):
    dp = lax.axis_index("dp")
    pr = lax.axis_index("proto")
    x, core = lax.div(dp, 2), lax.rem(dp, 2)
    y, z = lax.div(pr, NZ), lax.rem(pr, NZ)
    x_next, x_prev, x_far = lax.rem(x + 1, 4), lax.rem(x + 3, 4), lax.rem(x + 2, 4)
    right = (x_next * 2 + core, pr)
    left = (x_prev * 2 + core, pr)
    partner = (x * 2 + 1 - core, pr)

    def dp_peer(k):
        return (lax.rem(dp + k, 8), pr)

    def proto_peer(dy, dz):
        return (dp, lax.rem(y + dy, NY) * NZ + lax.rem(z + dz, NZ))

    def remote(src, dst, ssem, rsem, device):
        return pltpu.make_async_remote_copy(
            src, dst, ssem, rsem, device_id=device, device_id_type=MESH
        )

    def wait_bytes(ref, sem):
        pltpu.make_async_copy(ref, ref, sem).wait()

    def load(src, dst, sem, parts):
        size = src.shape[0] // parts
        for i in range(parts):
            rows = pl.ds(i * size, size)
            pltpu.make_async_copy(src.at[rows], dst.at[rows], sem).start()

    load(index_hbm, index_v, in_sem.at[0], 1)
    for j in range(4):
        cols = pl.ds(2 * W * j, 2 * W)
        pltpu.make_async_copy(protos_hbm.at[:, cols], protos_v.at[j], protos_sem.at[j]).start()
        if j == 0:
            load(teacher_hbm, teacher_v, in_sem.at[1], 4)
    load(student_hbm, student_v, in_sem.at[3], 4)
    barrier = pltpu.get_barrier_semaphore()
    for k in range(1, 8):
        pl.semaphore_signal(barrier, inc=1, device_id=dp_peer(k), device_id_type=MESH)
    for dy, dz in FAR_FIRST:
        pl.semaphore_signal(
            barrier, inc=1, device_id=proto_peer(dy, dz), device_id_type=MESH
        )

    wait_bytes(index_v, in_sem.at[0])
    for i in range(4):
        places = lax.broadcasted_iota(jnp.int32, (256, 128), 0)
        onehot[i] = jnp.where(places == index_v[i : i + 1, :], 1.0, 0.0).astype(BF16)

    def masked(patches, i):
        rows = lax.dot_general(
            onehot[i], patches[256 * i : 256 * i + 256, :],
            (((0,), (0,)), ((), ())), preferred_element_type=F32,
        )
        norm = jnp.sqrt(jnp.sum(rows * rows, axis=1, keepdims=True) + epsilon)
        return rows / norm, norm

    def norm_piece(q):
        wait_bytes(protos_v.at[q], protos_sem.at[q])
        for i in range(2):
            cols = pl.ds(pl.multiple_of((2 * q + i) * W, W), W)
            weights = protos_v[q, :, W * i : W * i + W].astype(F32)
            inv = 1.0 / jnp.sqrt(jnp.sum(weights * weights, axis=0, keepdims=True) + epsilon)
            pinv[:, cols] = inv
            pc[:, cols] = (weights * inv).astype(BF16)

    norm_piece(0)
    wait_bytes(teacher_v, in_sem.at[1])
    for i in range(4):
        unit, _ = masked(teacher_v, i)
        t_send[128 * i : 128 * i + 128, :] = unit
        t_cast[128 * i : 128 * i + 128, :] = unit.astype(BF16)

    def put_cols(buf, slot, j, sums):
        for q in range(W // 128):
            buf[slot, pl.ds(4 * j + q, 1), :] = sums[:, 128 * q : 128 * q + 128]


    def send_cols(t, q):
        piece = cbuf.at[t, dp, pl.ds(pl.multiple_of(8 * q, 8), 8)]
        for k in (4, 3, 5, 2, 6, 1, 7):
            remote(piece, piece, c_ssem, c_rsem.at[t, q // 2], dp_peer(k)).start()

    def take_cols(t, h):
        wait_bytes(cbuf.at[t, pl.ds(0, 7), pl.ds(16 * h, 16)], c_rsem.at[t, h])
        rows = slice(16 * h, 16 * h + 16)
        vrow[rows, :] = 1.0 / jnp.sum(cbuf[t, :, rows, :], axis=0)

    def score_piece(q):
        for i in range(2):
            j = 2 * q + i
            cols = pl.ds(pl.multiple_of(j * W, W), W)
            block = jnp.exp2(dot(t_cast[...], pc[:, cols]) * teacher_scale)
            expos[:, cols] = block
            put_cols(cbuf.at[0], dp, j, jnp.sum(block, axis=0, keepdims=True))

    def front(q, carry):
        norm_piece(q + 1)
        score_piece(q)
        return carry

    def low_part(q, carry):
        for i in range(2):
            cols = pl.ds(pl.multiple_of((2 * q + i) * W, W), W)
            unit = protos_v[q, :, W * i : W * i + W].astype(F32) * pinv[:, cols]
            plo[:, cols] = (unit - pc[:, cols].astype(F32)).astype(BF16)
        return carry

    lax.fori_loop(0, 3, front, 0)
    score_piece(3)
    pl.semaphore_wait(barrier, 7 + len(FAR_FIRST))
    for q in range(4):
        send_cols(0, q)

    def send_rows(t):
        for dy, dz in FAR_FIRST:
            remote(rbuf.at[t, pr], rbuf.at[t, pr], r_ssem, r_rsem.at[t], proto_peer(dy, dz)).start()

    def take_rows(t):
        wait_bytes(rbuf.at[t, pl.ds(0, 31)], r_rsem.at[t])
        return jnp.sum(rbuf[t], axis=0)

    def spread(row):
        return jnp.transpose(jnp.broadcast_to(row, (128, 128)))

    def row_pass(t):
        take_cols(t, 0)
        for i in range(4):
            rows = slice(128 * i, 128 * i + 128)
            total = expos[rows, 0:128] * vrow[0:1, :]
            for k in range(1, 16):
                total += expos[rows, 128 * k : 128 * k + 128] * vrow[k : k + 1, :]
            row_acc[rows, :] = total
        take_cols(t, 1)
        for i in range(4):
            rows = slice(128 * i, 128 * i + 128)
            total = row_acc[rows, :]
            for k in range(16, 32):
                total += expos[rows, 128 * k : 128 * k + 128] * vrow[k : k + 1, :]
            rbuf[t, pr, i : i + 1, :] = jnp.sum(jnp.transpose(total), axis=0, keepdims=True)

    def col_pass(t):
        def chunk(j, carry):
            cols = pl.ds(pl.multiple_of(j * 1024, 1024), 1024)
            sums = jnp.zeros((8, 1024), F32)
            for i in range(64):
                scale = ub[8 * i : 8 * i + 8, :]
                sums += expos[8 * i : 8 * i + 8, cols] * jnp.concatenate([scale] * 8, axis=1)
            total = jnp.sum(sums, axis=0, keepdims=True)
            for q in range(8):
                cbuf[t, dp, pl.ds(8 * j + q, 1), :] = total[:, 128 * q : 128 * q + 128]
            send_cols(t, j)
            return carry

        lax.fori_loop(0, 4, chunk, 0)

    def spread_rows(values, target):
        for i in range(4):
            target[128 * i : 128 * i + 128, :] = spread(values[i : i + 1, :])

    wait_bytes(student_v, in_sem.at[3])
    for i in range(4):
        unit, norm = masked(student_v, i)
        rows = slice(128 * i, 128 * i + 128)
        s_send[rows, :] = unit
        s_cast[rows, :] = unit.astype(BF16)
        s_inv[rows, :] = jnp.broadcast_to(1.0 / norm, (128, 128))
        s_unit_t[:, rows] = jnp.transpose(unit)
    ts = [
        remote(t_send, t_other, ts_ssem.at[0], ts_rsem.at[0], partner),
        remote(s_send, s_other, ts_ssem.at[1], ts_rsem.at[1], partner),
    ]
    for copy in ts:
        copy.start()

    half = core * 2048
    tot_acc[...] = jnp.zeros_like(tot_acc)
    fp[...] = jnp.zeros_like(fp)

    def student_cols(j, keep):
        at = lax.rem(j * W + half, 4096)
        cols = pl.ds(pl.multiple_of(at, W), W)
        block = jnp.exp2(dot(s_cast[...], pc[:, cols]) * student_scale)
        for q in range(W // 128):
            tot_acc[...] += block[:, 128 * q : 128 * q + 128]
        high, low = split(block)
        if keep:
            mine = pl.ds(pl.multiple_of(j * W, W), W)
            x2h[0:512, mine] = high
            x2l[0:512, mine] = low
        fp[...] += (
            dot_cols(high, pc[:, cols]) + dot_cols(low, pc[:, cols]) + dot_cols(high, plo[:, cols])
        )

    def student_mine(j, carry):
        student_cols(j, True)
        return carry

    def student_rest(j, carry):
        student_cols(j, False)
        return carry

    lax.fori_loop(0, 4, low_part, 0)
    lax.fori_loop(0, 2, student_mine, 0)
    row_pass(0)
    send_rows(0)

    lax.fori_loop(2, 4, student_mine, 0)
    lax.fori_loop(4, 8, student_rest, 0)
    for i in range(4):
        rbuf[3, pr, i : i + 1, :] = jnp.sum(
            jnp.transpose(tot_acc[128 * i : 128 * i + 128, :]), axis=0, keepdims=True
        )
    send_rows(3)
    spread_rows(1.0 / take_rows(0), ub)
    col_pass(1)

    def send_y(q, src, steps):
        for dy in steps:
            ty = lax.rem(y + dy, NY)
            remote(
                src.at[pl.ds(pl.multiple_of(ty * 128, 128), 128)], yr.at[q, dy - 1],
                y_ssem.at[q], y_rsem.at[q], proto_peer(dy, 0),
            ).start()

    def take_y(q, src):
        wait_bytes(yr.at[q], y_rsem.at[q])
        own = pl.ds(pl.multiple_of(y * 128, 128), 128)
        ysum[q] = src[own, :] + yr[q, 0] + yr[q, 1] + yr[q, 2]

    def send_z(q):
        for dz in (4, 3, 5, 2, 6, 1, 7):
            tz = lax.rem(z + dz, NZ)
            remote(
                ysum.at[q, pl.ds(pl.multiple_of(tz * 16, 16), 16)], zr.at[q, dz - 1],
                z_ssem, z_rsem.at[q], proto_peer(0, dz),
            ).start()

    def take_z(q):
        wait_bytes(zr.at[q], z_rsem.at[q])
        total = ysum[q, pl.ds(pl.multiple_of(z * 16, 16), 16), :]
        for k in range(7):
            total += zr[q, k]
        return total

    send_y(0, fp, (2,))
    for copy in ts:
        copy.wait_recv()
    t_cast[...] = t_other[...].astype(BF16)
    s_cast[...] = s_other[...].astype(BF16)

    def other_cols(j, carry):
        cols = pl.ds(pl.multiple_of(j * W + half, W), W)
        mine = pl.ds(pl.multiple_of(j * W, W), W)
        high, low = split(jnp.exp2(dot(t_cast[...], pc[:, cols]) * teacher_scale))
        e2h[512:1024, mine] = high
        e2l[512:1024, mine] = low
        high, low = split(jnp.exp2(dot(s_cast[...], pc[:, cols]) * student_scale))
        x2h[512:1024, mine] = high
        x2l[512:1024, mine] = low
        return carry

    lax.fori_loop(0, 4, other_cols, 0)
    row_pass(1)
    send_rows(1)

    def scale_half(at, ref):
        for i in range(4):
            cols = slice(at + 128 * i, at + 128 * i + 128)
            high, low = split(s_unit_t[:, cols] * ref[i : i + 1, :])
            a_hi[:, cols] = high
            a_lo[:, cols] = low

    def weigh(high, low, cols):
        return (
            dot(a_hi[...], high[:, cols]) + dot(a_lo[...], high[:, cols]) + dot(a_hi[...], low[:, cols])
        )

    tot_row[...] = 1.0 / take_rows(3)
    swap_s[0] = tot_row[...]
    swap_tot = remote(swap_s.at[0], swap_r.at[0], swap_ssem.at[0], swap_rsem.at[0], partner)
    swap_tot.start()
    spread_rows(tot_row[...], totb)
    def own_split(j, carry):
        cols = pl.ds(pl.multiple_of(j * W + half, W), W)
        mine = pl.ds(pl.multiple_of(j * W, W), W)
        high, low = split(expos[:, cols])
        e2h[0:512, mine] = high
        e2l[0:512, mine] = low
        return carry

    lax.fori_loop(0, 4, own_split, 0)
    for i in range(4):
        s_unit_t[:, 512 + 128 * i : 640 + 128 * i] = jnp.transpose(
            s_other[128 * i : 128 * i + 128, :]
        )
    scale_half(0, tot_row)
    swap_tot.wait_recv()
    scale_half(512, swap_r.at[0])

    def probs_part(j, carry):
        mine = pl.ds(pl.multiple_of(j * W, W), W)
        wtp[:, mine] = weigh(x2h, x2l, mine)
        return carry

    lax.fori_loop(0, 4, probs_part, 0)
    spread_rows(1.0 / take_rows(1), ub)
    col_pass(2)

    send_y(0, fp, (1, 3))
    row_pass(2)
    send_rows(2)

    ft[...] = jnp.zeros_like(ft)

    def target_cols(j, carry):
        cols = pl.ds(pl.multiple_of(j * W, W), W)
        unit = pc[:, cols].astype(F32) + plo[:, cols].astype(F32)
        scaled = jnp.concatenate(
            [
                unit[:, 128 * q : 128 * q + 128] * vrow[pl.ds(4 * j + q, 1), :]
                for q in range(W // 128)
            ],
            axis=1,
        )
        b_high, b_low = split(scaled)
        high, low = split(expos[:, cols])
        ft[...] += dot_cols(high, b_high) + dot_cols(low, b_high) + dot_cols(high, b_low)
        return carry

    lax.fori_loop(0, 4, target_cols, 0, unroll=2)
    take_y(0, fp)
    send_z(0)
    lax.fori_loop(4, 8, target_cols, 0, unroll=2)
    for n, dz in enumerate(Z_FAR_FIRST):
        tz = lax.rem(z + dz, NZ) * 16
        for dy in (2, 1, 3):
            ty = lax.rem(y + dy, NY) * 128
            remote(
                ft.at[pl.ds(pl.multiple_of(ty + tz, 16), 16)], yr.at[1, dy - 1, pl.ds(pl.multiple_of(tz, 16), 16)],
                yp_ssem, yp_rsem.at[n // 4], proto_peer(dy, 0),
            ).start()
    swap_s[1] = 1.0 / take_rows(2)
    swap_u = remote(swap_s.at[1], swap_r.at[1], swap_ssem.at[1], swap_rsem.at[1], partner)
    swap_u.start()
    def block(d, offset, size):
        return pl.ds(pl.multiple_of(d * 64 + offset, 32), size)

    def protos_part(j, target):
        mine = pl.ds(pl.multiple_of(j * V, V), V)
        cols = pl.ds(pl.multiple_of(j * V + half, V), V)
        at = half // 128 + V // 128 * j
        target = jnp.concatenate(
            [
                target[:, 128 * q : 128 * q + 128] * vrow[pl.ds(at + q, 1), :]
                for q in range(V // 128)
            ],
            axis=1,
        )
        total = wtp[:, mine] - target
        unit = pc[:, cols].astype(F32) + plo[:, cols].astype(F32)
        inner = jnp.sum(unit * total, axis=0, keepdims=True)
        gpart[j] = (total - unit * inner) * (pinv[:, cols] * slope_scale)
        remote(gpart.at[j, block(x_far, 0, 32)], p1r.at[j, 0], p1_ssem, p1_rsem.at[j], right).start()
        remote(gpart.at[j, block(x_far, 32, 32)], p1r.at[j, 1], p1_ssem, p1_rsem.at[j], left).start()
        remote(gpart.at[j, block(x, 32 - 32 * core, 32)], p2r.at[j, 4], p2_ssem, p2_rsem.at[j], partner).start()

    def weigh_some(rows, cols):
        return (
            dot(a_hi[:, rows], e2h[rows, cols])
            + dot(a_lo[:, rows], e2h[rows, cols])
            + dot(a_hi[:, rows], e2l[rows, cols])
        )

    first = pl.ds(0, V)
    scale_half(0, swap_s.at[1])
    target = weigh_some(slice(0, 512), first)
    swap_u.wait_recv()
    scale_half(512, swap_r.at[1])
    protos_part(0, target + weigh_some(slice(512, 1024), first))

    def protos_rest(j, carry):
        protos_part(j, weigh(e2h, e2l, pl.ds(pl.multiple_of(j * V, V), V)))
        return carry

    def take_pieces(first, last):
        wait_bytes(yr.at[1, pl.ds(0, 3), pl.ds(0, 64)], yp_rsem.at[first // 4])
        for dz in Z_FAR_FIRST[first:last]:
            tz = lax.rem(z + dz, NZ) * 16
            rows = pl.ds(pl.multiple_of(tz, 16), 16)
            own = pl.ds(pl.multiple_of(y * 128 + tz, 16), 16)
            ysum[1, rows, :] = ft[own, :] + yr[1, 0, rows, :] + yr[1, 1, rows, :] + yr[1, 2, rows, :]
            if dz:
                remote(
                    ysum.at[1, rows], zr.at[1, dz - 1], z_ssem, z_rsem.at[1], proto_peer(0, dz)
                ).start()

    def pass_on(j, carry):
        wait_bytes(p1r.at[j], p1_rsem.at[j])
        for s, side in enumerate((x_next, x_prev)):
            gpart[j, block(side, 32 * s, 32), :] += p1r[j, s]
            for c in range(2):
                remote(
                    gpart.at[j, block(side, 32 * c, 32)], p2r.at[j, 2 * s + core],
                    p2_ssem, p2_rsem.at[j], (side * 2 + c, pr),
                ).start()
        return carry

    lax.fori_loop(1, 5, protos_rest, 0)
    pass_on(0, 0)
    take_pieces(0, 4)
    lax.fori_loop(5, 8, protos_rest, 0)

    lax.fori_loop(1, 4, pass_on, 0)
    take_pieces(4, 8)
    lax.fori_loop(4, 6, pass_on, 0)
    spread_rows(swap_s[1], ub)

    own16 = pl.ds(pl.multiple_of(y * 128 + z * 16, 16), 16)
    by_probs = take_z(0)
    by_target = take_z(1)
    unit = s_send[own16, :]
    scale_p = jnp.concatenate([totb[own16, :]] * 2, axis=1)
    scale_t = jnp.concatenate([ub[own16, :]] * 2, axis=1)
    grad = slope_scale * (by_probs * scale_p - by_target * scale_t)
    inner = jnp.sum(unit * grad, axis=1, keepdims=True)
    ag[y, z] = (grad - unit * inner) * jnp.concatenate([s_inv[own16, :]] * 2, axis=1)
    for dz in (1, 7, 2, 6, 3, 5, 4):
        remote(ag.at[y, z], ag.at[y, z], agz_ssem, agz_rsem.at[dz - 1], proto_peer(0, dz)).start()

    def to_y(piece):
        for dy in (2, 1, 3):
            remote(piece, piece, agy_ssem, agy_rsem.at[dy - 1], proto_peer(dy, 0)).start()

    to_y(ag.at[y, z])
    lax.fori_loop(6, 8, pass_on, 0)

    def finish(j, carry):
        wait_bytes(p2r.at[j], p2_rsem.at[j])
        gw_ref[j, 0] = gpart[j, block(x, 32 * core, 32), :] + p2r[j, core] + p2r[j, 2 + core]
        gw_ref[j, 1] = p2r[j, 4] + p2r[j, 1 - core] + p2r[j, 3 - core]
        for i, start in enumerate((half, 2048 - half)):
            cols = pl.ds(pl.multiple_of(j * V + start, V), V)
            pltpu.make_async_copy(gw_ref.at[j, i], gw_hbm.at[:, cols], out_sem.at[0]).start()
        return carry

    for dz in (1, 7, 2, 6, 3, 5, 4):
        piece = ag.at[y, lax.rem(z + NZ - dz, NZ)]
        wait_bytes(piece, agz_rsem.at[dz - 1])
        to_y(piece)
    pltpu.make_async_copy(ag.at[y], rows_hbm.at[y], out_sem.at[1]).start()
    lax.fori_loop(0, 8, finish, 0)

    for dy in (1, 3, 2):
        image = lax.rem(y + NY - dy, NY)
        wait_bytes(ag.at[image], agy_rsem.at[dy - 1])
        pltpu.make_async_copy(ag.at[image], rows_hbm.at[image], out_sem.at[1]).start()

    wait_bytes(cbuf.at[:, pl.ds(0, 7)], c_ssem)
    wait_bytes(rbuf.at[:, pl.ds(0, 31)], r_ssem)
    for copy in ts:
        copy.wait_send()
    swap_tot.wait_send()
    swap_u.wait_send()
    wait_bytes(yr.at[0], y_ssem.at[0])
    wait_bytes(yr.at[1], yp_ssem)
    wait_bytes(zr, z_ssem)
    wait_bytes(ag.at[0, pl.ds(0, 7)], agz_ssem)
    wait_bytes(ag.at[pl.ds(0, 3)], agy_ssem)

    wait_bytes(p1r, p1_ssem)
    wait_bytes(p2r, p2_ssem)
    wait_bytes(gw_ref, out_sem.at[0])
    wait_bytes(ag, out_sem.at[1])


def place_kernel(rows_hbm, index_hbm, gw_in, gp_hbm, gw_hbm, rows, index, placed, gw, sem, out_sem):
    gw_load = pltpu.make_async_copy(gw_in, gw, sem.at[5])
    loads = [pltpu.make_async_copy(index_hbm, index, sem.at[4])]
    loads += [pltpu.make_async_copy(rows_hbm.at[i], rows.at[i], sem.at[i]) for i in range(4)]
    for copy in [*loads, gw_load]:
        copy.start()
    loads[0].wait()
    onehots = []
    for i in range(4):
        places = lax.broadcasted_iota(jnp.int32, (256, 128), 0)
        onehots.append(jnp.where(places == index[i : i + 1, :], 1.0, 0.0).astype(BF16))
    for copy in loads[1:]:
        copy.wait()
    stores = []
    for i in range(4):
        value = rows[i]
        high, low = split(value)
        rest = (value - high.astype(F32) - low.astype(F32)).astype(BF16)
        placed[i] = dot(onehots[i], high) + dot(onehots[i], low) + dot(onehots[i], rest)
        stores.append(
            pltpu.make_async_copy(placed.at[i], gp_hbm.at[pl.ds(256 * i, 256)], out_sem.at[i])
        )
        stores[-1].start()
        if i == 0:
            gw_load.wait()
            stores.append(pltpu.make_async_copy(gw, gw_hbm, out_sem.at[4]))
            stores[-1].start()
    for copy in stores:
        copy.wait()


def body(student_patches, teacher_patches, masked_index, prototypes):
    dma = pltpu.SemaphoreType.DMA

    def vmem(*shape, dtype=F32):
        return pltpu.VMEM(shape, dtype)

    def half_vmem(*shape):
        return pltpu.VMEM(shape, BF16)

    scratch = [
        half_vmem(1024, 256), half_vmem(1024, 256), vmem(4, 128, dtype=jnp.int32), half_vmem(4, 256, 1024), dma((4,)), dma((4,)),
        half_vmem(4, 256, 128), vmem(512, 256), vmem(512, 256), vmem(512, 256), vmem(512, 256),
        half_vmem(512, 256), half_vmem(512, 256), vmem(256, 1024), vmem(512, 128),
        half_vmem(256, 4096), half_vmem(256, 4096), vmem(1, 4096), vmem(512, 4096),
        half_vmem(1024, 2048), half_vmem(1024, 2048), half_vmem(1024, 2048), half_vmem(1024, 2048),
        vmem(256, 2048), half_vmem(256, 1024), half_vmem(256, 1024),
        vmem(3, 8, 32, 128), dma, dma((3, 2)),
        vmem(4, 32, 4, 128), dma, dma((4,)),
        vmem(512, 128), vmem(512, 128), vmem(32, 128), vmem(4, 128), vmem(512, 128), vmem(512, 128),
        dma((2,)), dma((2,)), vmem(2, 4, 128), vmem(2, 4, 128), dma((2,)), dma((2,)),
        vmem(512, 256), vmem(512, 256), vmem(2, 3, 128, 256), vmem(2, 128, 256), dma((1,)), dma((1,)), dma, dma((2,)),
        vmem(2, 7, 16, 256), dma, dma((2,)),
        vmem(4, 8, 16, 256), dma, dma((7,)), dma, dma((3,)),
        vmem(8, 256, 256), vmem(8, 2, 32, 256), dma, dma((8,)),
        vmem(8, 5, 32, 256), dma, dma((8,)), vmem(8, 2, 32, 256), dma((2,)),
    ]
    anywhere = pl.BlockSpec(memory_space=pl.ANY)
    rows, grad_prototypes = pl.pallas_call(
        kernel,
        out_shape=(
            jax.ShapeDtypeStruct((4, 8, 16, 256), F32),
            jax.ShapeDtypeStruct((32, 4096), F32),
        ),
        in_specs=[anywhere] * 4,
        out_specs=(anywhere, anywhere),
        scratch_shapes=scratch,
        compiler_params=pltpu.CompilerParams(
            collective_id=0, has_side_effects=True, vmem_limit_bytes=60 * 1024 * 1024
        ),
    )(student_patches, teacher_patches, masked_index, prototypes)
    return pl.pallas_call(
        place_kernel,
        out_shape=(
            jax.ShapeDtypeStruct((1024, 256), F32),
            jax.ShapeDtypeStruct((32, 4096), F32),
        ),
        in_specs=[anywhere] * 3,
        out_specs=(anywhere, anywhere),
        scratch_shapes=[
            vmem(4, 128, 256), vmem(4, 128, dtype=jnp.int32), vmem(4, 256, 256), vmem(32, 4096), dma((6,)), dma((5,)),
        ],
    )(rows.reshape(4, 128, 256), masked_index, grad_prototypes)


def solution(mesh):
    placed = (P("dp", None), P("dp", None), P("dp", None), P(None, "proto"))
    return jax.shard_map(
        body,
        mesh=mesh,
        in_specs=placed,
        out_specs=(P("dp", None), P("dp", "proto")),
        check_vma=False,
    )
```

time: 73.8 us -> 69.3 us (0.939)
  Pallas kernels: 73 us -> 68.5 us
    pallas_call x1, Pallas kernels: 69.3 us -> 65.7 us  [body(): pl.pallas_call(kernel, out_shape=(jax.ShapeDtypeStruct((4, 8, 16, 256), F...]
    pallas_call x1, Pallas kernels: 3.78 us -> 2.8 us  [body(): pl.pallas_call(place_kernel, out_shape=(jax.ShapeDtypeStruct((1024, 256),...]
where the time goes in v3:
time: 69.3 us; the launch traced here: 69.1 us
  Pallas kernels  68.5 us (99%)
    pallas_call x1, Pallas kernels, body(): pl.pallas_call(kernel, out_shape=(jax.ShapeDtypeStruct((4, 8, 16, 256), F...  65.7 us
    pallas_call x1, Pallas kernels, body(): pl.pallas_call(place_kernel, out_shape=(jax.ShapeDtypeStruct((1024, 256),...  2.8 us

profile of v3, /device:TPU:1, one launch (start us, length us, event | category | flops | bytes accessed | tf_op | source)
XLA Modules:
  0.0 69.1 jit_solution(5070424860807427028)
XLA Ops:
  0.6 65.7 %shard_map.59 = (f32[4,8,16,256]{3,2,1,0:T(8,128)}, f32[32,4096]{1,0:T(8,128)}) custom-call(bf16[1024,256]{1,0:T(8,128)(2,1)} %student_hbm.1, bf16[1024,256]{1,0:T(8,128)(2,1)} %teacher_hbm.1, s32[4,128]{1,0:T(4,128)} %index_hbm.3, bf16[256,4096]{1,0:T(8,128)(2,1)} %protos_hbm.1), custom_call_target="tpu_custom_call" | custom-call | tf_op jit(solution)/shard_map/pallas_call | solution.py:591
  66.3 2.8 %shard_map.60 = (f32[1024,256]{1,0:T(8,128)}, f32[32,4096]{1,0:T(8,128)}) custom-call(f32[4,128,256]{2,1,0:T(8,128)} %bitcast.1, s32[4,128]{1,0:T(4,128)} %index_hbm.3, f32[32,4096]{1,0:T(8,128)} %get-tuple-element.5.gw_in), custom_call_target="tpu_custom_call" | custom-call | tf_op jit(solution)/shard_map/pallas_call | solution.py:604

commit v4 on v3

--- a/solution.py
+++ b/solution.py
@@ -84,11 +84,10 @@
             pltpu.make_async_copy(src.at[rows], dst.at[rows], sem).start()
 
     load(index_hbm, index_v, in_sem.at[0], 1)
+    load(teacher_hbm, teacher_v, in_sem.at[1], 4)
     for j in range(4):
         cols = pl.ds(2 * W * j, 2 * W)
         pltpu.make_async_copy(protos_hbm.at[:, cols], protos_v.at[j], protos_sem.at[j]).start()
-        if j == 0:
-            load(teacher_hbm, teacher_v, in_sem.at[1], 4)
     load(student_hbm, student_v, in_sem.at[3], 4)
     barrier = pltpu.get_barrier_semaphore()
     for k in range(1, 8):
@@ -111,16 +110,6 @@
         norm = jnp.sqrt(jnp.sum(rows * rows, axis=1, keepdims=True) + epsilon)
         return rows / norm, norm
 
-    def norm_piece(q):
-        wait_bytes(protos_v.at[q], protos_sem.at[q])
-        for i in range(2):
-            cols = pl.ds(pl.multiple_of((2 * q + i) * W, W), W)
-            weights = protos_v[q, :, W * i : W * i + W].astype(F32)
-            inv = 1.0 / jnp.sqrt(jnp.sum(weights * weights, axis=0, keepdims=True) + epsilon)
-            pinv[:, cols] = inv
-            pc[:, cols] = (weights * inv).astype(BF16)
-
-    norm_piece(0)
     wait_bytes(teacher_v, in_sem.at[1])
     for i in range(4):
         unit, _ = masked(teacher_v, i)
@@ -135,24 +124,26 @@
     def send_cols(t, q):
         piece = cbuf.at[t, dp, pl.ds(pl.multiple_of(8 * q, 8), 8)]
         for k in (4, 3, 5, 2, 6, 1, 7):
-            remote(piece, piece, c_ssem, c_rsem.at[t, q // 2], dp_peer(k)).start()
-
-    def take_cols(t, h):
-        wait_bytes(cbuf.at[t, pl.ds(0, 7), pl.ds(16 * h, 16)], c_rsem.at[t, h])
-        rows = slice(16 * h, 16 * h + 16)
+            remote(piece, piece, c_ssem, c_rsem.at[t, q], dp_peer(k)).start()
+
+    def take_cols(t, q):
+        rows = slice(8 * q, 8 * q + 8)
+        wait_bytes(cbuf.at[t, pl.ds(0, 7), rows], c_rsem.at[t, q])
         vrow[rows, :] = 1.0 / jnp.sum(cbuf[t, :, rows, :], axis=0)
 
-    def score_piece(q):
+    def front(q, carry):
+        wait_bytes(protos_v.at[q], protos_sem.at[q])
         for i in range(2):
             j = 2 * q + i
             cols = pl.ds(pl.multiple_of(j * W, W), W)
-            block = jnp.exp2(dot(t_cast[...], pc[:, cols]) * teacher_scale)
+            weights = protos_v[q, :, W * i : W * i + W].astype(F32)
+            inv = 1.0 / jnp.sqrt(jnp.sum(weights * weights, axis=0, keepdims=True) + epsilon)
+            pinv[:, cols] = inv
+            unit = (weights * inv).astype(BF16)
+            pc[:, cols] = unit
+            block = jnp.exp2(dot(t_cast[...], unit) * teacher_scale)
             expos[:, cols] = block
             put_cols(cbuf.at[0], dp, j, jnp.sum(block, axis=0, keepdims=True))
-
-    def front(q, carry):
-        norm_piece(q + 1)
-        score_piece(q)
         return carry
 
     def low_part(q, carry):
@@ -162,8 +153,7 @@
             plo[:, cols] = (unit - pc[:, cols].astype(F32)).astype(BF16)
         return carry
 
-    lax.fori_loop(0, 3, front, 0)
-    score_piece(3)
+    lax.fori_loop(0, 4, front, 0)
     pl.semaphore_wait(barrier, 7 + len(FAR_FIRST))
     for q in range(4):
         send_cols(0, q)
@@ -180,20 +170,19 @@
         return jnp.transpose(jnp.broadcast_to(row, (128, 128)))
 
     def row_pass(t):
-        take_cols(t, 0)
-        for i in range(4):
-            rows = slice(128 * i, 128 * i + 128)
-            total = expos[rows, 0:128] * vrow[0:1, :]
-            for k in range(1, 16):
-                total += expos[rows, 128 * k : 128 * k + 128] * vrow[k : k + 1, :]
-            row_acc[rows, :] = total
-        take_cols(t, 1)
-        for i in range(4):
-            rows = slice(128 * i, 128 * i + 128)
-            total = row_acc[rows, :]
-            for k in range(16, 32):
-                total += expos[rows, 128 * k : 128 * k + 128] * vrow[k : k + 1, :]
-            rbuf[t, pr, i : i + 1, :] = jnp.sum(jnp.transpose(total), axis=0, keepdims=True)
+        for p in range(4):
+            take_cols(t, p)
+            for i in range(4):
+                rows = slice(128 * i, 128 * i + 128)
+                total = row_acc[rows, :] if p else jnp.zeros((128, 128), F32)
+                for k in range(8 * p, 8 * p + 8):
+                    total += expos[rows, 128 * k : 128 * k + 128] * vrow[k : k + 1, :]
+                if p < 3:
+                    row_acc[rows, :] = total
+                else:
+                    rbuf[t, pr, i : i + 1, :] = jnp.sum(
+                        jnp.transpose(total), axis=0, keepdims=True
+                    )
 
     def col_pass(t):
         def chunk(j, carry):
@@ -317,6 +306,10 @@
         return carry
 
     lax.fori_loop(0, 4, other_cols, 0)
+    for i in range(4):
+        s_unit_t[:, 512 + 128 * i : 640 + 128 * i] = jnp.transpose(
+            s_other[128 * i : 128 * i + 128, :]
+        )
     row_pass(1)
     send_rows(1)
 
@@ -327,16 +320,39 @@
             a_hi[:, cols] = high
             a_lo[:, cols] = low
 
-    def weigh(high, low, cols):
-        return (
-            dot(a_hi[...], high[:, cols]) + dot(a_lo[...], high[:, cols]) + dot(a_hi[...], low[:, cols])
-        )
-
     tot_row[...] = 1.0 / take_rows(3)
     swap_s[0] = tot_row[...]
     swap_tot = remote(swap_s.at[0], swap_r.at[0], swap_ssem.at[0], swap_rsem.at[0], partner)
     swap_tot.start()
     spread_rows(tot_row[...], totb)
+    def weigh_some(rows, cols, high, low):
+        return (
+            dot(a_hi[:, rows], high[rows, cols])
+            + dot(a_lo[:, rows], high[rows, cols])
+            + dot(a_hi[:, rows], low[rows, cols])
+        )
+
+    scale_half(0, tot_row)
+
+    def probs_own(j, carry):
+        mine = pl.ds(pl.multiple_of(j * W, W), W)
+        wtp[:, mine] = weigh_some(slice(0, 512), mine, x2h, x2l)
+        return carry
+
+    lax.fori_loop(0, 4, probs_own, 0)
+    swap_tot.wait_recv()
+    scale_half(512, swap_r.at[0])
+
+    def probs_other(j, carry):
+        mine = pl.ds(pl.multiple_of(j * W, W), W)
+        wtp[:, mine] += weigh_some(slice(512, 1024), mine, x2h, x2l)
+        return carry
+
+    lax.fori_loop(0, 4, probs_other, 0)
+    spread_rows(1.0 / take_rows(1), ub)
+    col_pass(2)
+
+    send_y(0, fp, (1, 3))
     def own_split(j, carry):
         cols = pl.ds(pl.multiple_of(j * W + half, W), W)
         mine = pl.ds(pl.multiple_of(j * W, W), W)
@@ -346,48 +362,34 @@
         return carry
 
     lax.fori_loop(0, 4, own_split, 0)
-    for i in range(4):
-        s_unit_t[:, 512 + 128 * i : 640 + 128 * i] = jnp.transpose(
-            s_other[128 * i : 128 * i + 128, :]
-        )
-    scale_half(0, tot_row)
-    swap_tot.wait_recv()
-    scale_half(512, swap_r.at[0])
-
-    def probs_part(j, carry):
-        mine = pl.ds(pl.multiple_of(j * W, W), W)
-        wtp[:, mine] = weigh(x2h, x2l, mine)
-        return carry
-
-    lax.fori_loop(0, 4, probs_part, 0)
-    spread_rows(1.0 / take_rows(1), ub)
-    col_pass(2)
-
-    send_y(0, fp, (1, 3))
     row_pass(2)
     send_rows(2)
 
     ft[...] = jnp.zeros_like(ft)
 
-    def target_cols(j, carry):
-        cols = pl.ds(pl.multiple_of(j * W, W), W)
-        unit = pc[:, cols].astype(F32) + plo[:, cols].astype(F32)
-        scaled = jnp.concatenate(
-            [
-                unit[:, 128 * q : 128 * q + 128] * vrow[pl.ds(4 * j + q, 1), :]
-                for q in range(W // 128)
-            ],
-            axis=1,
-        )
-        b_high, b_low = split(scaled)
-        high, low = split(expos[:, cols])
-        ft[...] += dot_cols(high, b_high) + dot_cols(low, b_high) + dot_cols(high, b_low)
-        return carry
-
-    lax.fori_loop(0, 4, target_cols, 0, unroll=2)
+    def target_cols(q, carry):
+        total = ft[...]
+        for i in range(2):
+            j = 2 * q + i
+            cols = pl.ds(pl.multiple_of(j * W, W), W)
+            inv = pinv[:, cols]
+            scale = jnp.concatenate(
+                [
+                    inv[:, 128 * n : 128 * n + 128] * vrow[pl.ds(4 * j + n, 1), :]
+                    for n in range(W // 128)
+                ],
+                axis=1,
+            )
+            b_high, b_low = split(protos_v[q, :, W * i : W * i + W].astype(F32) * scale)
+            high, low = split(expos[:, cols])
+            total += dot_cols(high, b_high) + dot_cols(low, b_high) + dot_cols(high, b_low)
+        ft[...] = total
+        return carry
+
+    lax.fori_loop(0, 2, target_cols, 0)
     take_y(0, fp)
     send_z(0)
-    lax.fori_loop(4, 8, target_cols, 0, unroll=2)
+    lax.fori_loop(2, 4, target_cols, 0)
     for n, dz in enumerate(Z_FAR_FIRST):
         tz = lax.rem(z + dz, NZ) * 16
         for dy in (2, 1, 3):
@@ -414,29 +416,23 @@
             axis=1,
         )
         total = wtp[:, mine] - target
-        unit = pc[:, cols].astype(F32) + plo[:, cols].astype(F32)
+        inside = pl.ds(pl.multiple_of(lax.rem(j, 4) * V, V), V)
+        unit = protos_v[2 * core + lax.div(j, 4), :, inside].astype(F32) * pinv[:, cols]
         inner = jnp.sum(unit * total, axis=0, keepdims=True)
         gpart[j] = (total - unit * inner) * (pinv[:, cols] * slope_scale)
         remote(gpart.at[j, block(x_far, 0, 32)], p1r.at[j, 0], p1_ssem, p1_rsem.at[j], right).start()
         remote(gpart.at[j, block(x_far, 32, 32)], p1r.at[j, 1], p1_ssem, p1_rsem.at[j], left).start()
         remote(gpart.at[j, block(x, 32 - 32 * core, 32)], p2r.at[j, 4], p2_ssem, p2_rsem.at[j], partner).start()
 
-    def weigh_some(rows, cols):
-        return (
-            dot(a_hi[:, rows], e2h[rows, cols])
-            + dot(a_lo[:, rows], e2h[rows, cols])
-            + dot(a_hi[:, rows], e2l[rows, cols])
-        )
-
     first = pl.ds(0, V)
     scale_half(0, swap_s.at[1])
-    target = weigh_some(slice(0, 512), first)
+    target = weigh_some(slice(0, 512), first, e2h, e2l)
     swap_u.wait_recv()
     scale_half(512, swap_r.at[1])
-    protos_part(0, target + weigh_some(slice(512, 1024), first))
+    protos_part(0, target + weigh_some(slice(512, 1024), first, e2h, e2l))
 
     def protos_rest(j, carry):
-        protos_part(j, weigh(e2h, e2l, pl.ds(pl.multiple_of(j * V, V), V)))
+        protos_part(j, weigh_some(slice(0, 1024), pl.ds(pl.multiple_of(j * V, V), V), e2h, e2l))
         return carry
 
     def take_pieces(first, last):
@@ -532,28 +528,26 @@
 
 def place_kernel(rows_hbm, index_hbm, gw_in, gp_hbm, gw_hbm, rows, index, placed, gw, sem, out_sem):
     gw_load = pltpu.make_async_copy(gw_in, gw, sem.at[5])
-    loads = [pltpu.make_async_copy(index_hbm, index, sem.at[4])]
-    loads += [pltpu.make_async_copy(rows_hbm.at[i], rows.at[i], sem.at[i]) for i in range(4)]
-    for copy in [*loads, gw_load]:
+    loads = [pltpu.make_async_copy(rows_hbm.at[i], rows.at[i], sem.at[i]) for i in range(4)]
+    index_load = pltpu.make_async_copy(index_hbm, index, sem.at[4])
+    for copy in [*loads, index_load, gw_load]:
         copy.start()
-    loads[0].wait()
+    index_load.wait()
     onehots = []
     for i in range(4):
         places = lax.broadcasted_iota(jnp.int32, (256, 128), 0)
         onehots.append(jnp.where(places == index[i : i + 1, :], 1.0, 0.0).astype(BF16))
-    for copy in loads[1:]:
+    for copy in loads:
         copy.wait()
     stores = []
     for i in range(4):
-        value = rows[i]
-        high, low = split(value)
-        rest = (value - high.astype(F32) - low.astype(F32)).astype(BF16)
-        placed[i] = dot(onehots[i], high) + dot(onehots[i], low) + dot(onehots[i], rest)
+        high, low = split(rows[i])
+        placed[i] = dot(onehots[i], high) + dot(onehots[i], low)
         stores.append(
             pltpu.make_async_copy(placed.at[i], gp_hbm.at[pl.ds(256 * i, 256)], out_sem.at[i])
         )
         stores[-1].start()
-        if i == 0:
+        if i == 1:
             gw_load.wait()
             stores.append(pltpu.make_async_copy(gw, gw_hbm, out_sem.at[4]))
             stores[-1].start()
@@ -577,7 +571,7 @@
         half_vmem(256, 4096), half_vmem(256, 4096), vmem(1, 4096), vmem(512, 4096),
         half_vmem(1024, 2048), half_vmem(1024, 2048), half_vmem(1024, 2048), half_vmem(1024, 2048),
         vmem(256, 2048), half_vmem(256, 1024), half_vmem(256, 1024),
-        vmem(3, 8, 32, 128), dma, dma((3, 2)),
+        vmem(3, 8, 32, 128), dma, dma((3, 4)),
         vmem(4, 32, 4, 128), dma, dma((4,)),
         vmem(512, 128), vmem(512, 128), vmem(32, 128), vmem(4, 128), vmem(512, 128), vmem(512, 128),
         dma((2,)), dma((2,)), vmem(2, 4, 128), vmem(2, 4, 128), dma((2,)), dma((2,)),

time: 69.3 us -> 68.5 us (0.988)
  Pallas kernels: 68.5 us -> 67.8 us
where the time goes in v4:
time: 68.5 us; the launch traced here: 68.4 us
  Pallas kernels  67.8 us (99%)
    pallas_call x1, Pallas kernels, body(): pl.pallas_call(kernel, out_shape=(jax.ShapeDtypeStruct((4, 8, 16, 256), F...  65.1 us
    pallas_call x1, Pallas kernels, body(): pl.pallas_call(place_kernel, out_shape=(jax.ShapeDtypeStruct((1024, 256),...  2.62 us

profile of v4, /device:TPU:1, one launch (start us, length us, event | category | flops | bytes accessed | tf_op | source)
XLA Modules:
  0.0 68.4 jit_solution(18149166196605758926)
XLA Ops:
  0.6 65.1 %shard_map.59 = (f32[4,8,16,256]{3,2,1,0:T(8,128)}, f32[32,4096]{1,0:T(8,128)}) custom-call(bf16[1024,256]{1,0:T(8,128)(2,1)} %student_hbm.1, bf16[1024,256]{1,0:T(8,128)(2,1)} %teacher_hbm.1, s32[4,128]{1,0:T(4,128)} %index_hbm.3, bf16[256,4096]{1,0:T(8,128)(2,1)} %protos_hbm.1), custom_call_target="tpu_custom_call" | custom-call | tf_op jit(solution)/shard_map/pallas_call | solution.py:585
  65.8 2.6 %shard_map.60 = (f32[1024,256]{1,0:T(8,128)}, f32[32,4096]{1,0:T(8,128)}) custom-call(f32[4,128,256]{2,1,0:T(8,128)} %bitcast.1, s32[4,128]{1,0:T(4,128)} %index_hbm.3, f32[32,4096]{1,0:T(8,128)} %get-tuple-element.5.gw_in), custom_call_target="tpu_custom_call" | custom-call | tf_op jit(solution)/shard_map/pallas_call | solution.py:598

commit v5 on v4

--- a/solution.py
+++ b/solution.py
@@ -85,10 +85,6 @@
 
     load(index_hbm, index_v, in_sem.at[0], 1)
     load(teacher_hbm, teacher_v, in_sem.at[1], 4)
-    for j in range(4):
-        cols = pl.ds(2 * W * j, 2 * W)
-        pltpu.make_async_copy(protos_hbm.at[:, cols], protos_v.at[j], protos_sem.at[j]).start()
-    load(student_hbm, student_v, in_sem.at[3], 4)
     barrier = pltpu.get_barrier_semaphore()
     for k in range(1, 8):
         pl.semaphore_signal(barrier, inc=1, device_id=dp_peer(k), device_id_type=MESH)
@@ -96,6 +92,10 @@
         pl.semaphore_signal(
             barrier, inc=1, device_id=proto_peer(dy, dz), device_id_type=MESH
         )
+    for j in range(4):
+        cols = pl.ds(2 * W * j, 2 * W)
+        pltpu.make_async_copy(protos_hbm.at[:, cols], protos_v.at[j], protos_sem.at[j]).start()
+    load(student_hbm, student_v, in_sem.at[3], 4)
 
     wait_bytes(index_v, in_sem.at[0])
     for i in range(4):
@@ -131,12 +131,13 @@
         wait_bytes(cbuf.at[t, pl.ds(0, 7), rows], c_rsem.at[t, q])
         vrow[rows, :] = 1.0 / jnp.sum(cbuf[t, :, rows, :], axis=0)
 
-    def front(q, carry):
-        wait_bytes(protos_v.at[q], protos_sem.at[q])
+    def front(p, carry):
         for i in range(2):
-            j = 2 * q + i
+            wait_bytes(protos_v.at[2 * p + i], protos_sem.at[2 * p + i])
+        for i in range(4):
+            j = 4 * p + i
             cols = pl.ds(pl.multiple_of(j * W, W), W)
-            weights = protos_v[q, :, W * i : W * i + W].astype(F32)
+            weights = protos_v[2 * p + i // 2, :, W * (i % 2) : W * (i % 2) + W].astype(F32)
             inv = 1.0 / jnp.sqrt(jnp.sum(weights * weights, axis=0, keepdims=True) + epsilon)
             pinv[:, cols] = inv
             unit = (weights * inv).astype(BF16)
@@ -153,7 +154,7 @@
             plo[:, cols] = (unit - pc[:, cols].astype(F32)).astype(BF16)
         return carry
 
-    lax.fori_loop(0, 4, front, 0)
+    lax.fori_loop(0, 2, front, 0)
     pl.semaphore_wait(barrier, 7 + len(FAR_FIRST))
     for q in range(4):
         send_cols(0, q)
@@ -526,31 +527,18 @@
     wait_bytes(ag, out_sem.at[1])
 
 
-def place_kernel(rows_hbm, index_hbm, gw_in, gp_hbm, gw_hbm, rows, index, placed, gw, sem, out_sem):
-    gw_load = pltpu.make_async_copy(gw_in, gw, sem.at[5])
-    loads = [pltpu.make_async_copy(rows_hbm.at[i], rows.at[i], sem.at[i]) for i in range(4)]
-    index_load = pltpu.make_async_copy(index_hbm, index, sem.at[4])
-    for copy in [*loads, index_load, gw_load]:
-        copy.start()
-    index_load.wait()
-    onehots = []
+def place_kernel(rows, index, gw, gp_hbm, gw_hbm, placed, out_sem):
+    stores = [pltpu.make_async_copy(gw, gw_hbm, out_sem.at[4])]
+    stores[0].start()
     for i in range(4):
         places = lax.broadcasted_iota(jnp.int32, (256, 128), 0)
-        onehots.append(jnp.where(places == index[i : i + 1, :], 1.0, 0.0).astype(BF16))
-    for copy in loads:
-        copy.wait()
-    stores = []
-    for i in range(4):
-        high, low = split(rows[i])
-        placed[i] = dot(onehots[i], high) + dot(onehots[i], low)
+        onehot = jnp.where(places == index[i : i + 1, :], 1.0, 0.0).astype(BF16)
+        high, low = split(rows[i].reshape(128, 256))
+        placed[i] = dot(onehot, high) + dot(onehot, low)
         stores.append(
             pltpu.make_async_copy(placed.at[i], gp_hbm.at[pl.ds(256 * i, 256)], out_sem.at[i])
         )
         stores[-1].start()
-        if i == 1:
-            gw_load.wait()
-            stores.append(pltpu.make_async_copy(gw, gw_hbm, out_sem.at[4]))
-            stores[-1].start()
     for copy in stores:
         copy.wait()
 
@@ -585,8 +573,8 @@
     rows, grad_prototypes = pl.pallas_call(
         kernel,
         out_shape=(
-            jax.ShapeDtypeStruct((4, 8, 16, 256), F32),
-            jax.ShapeDtypeStruct((32, 4096), F32),
+            pltpu.VMEM((4, 8, 16, 256), F32),
+            pltpu.VMEM((32, 4096), F32),
         ),
         in_specs=[anywhere] * 4,
         out_specs=(anywhere, anywhere),
@@ -601,12 +589,14 @@
             jax.ShapeDtypeStruct((1024, 256), F32),
             jax.ShapeDtypeStruct((32, 4096), F32),
         ),
-        in_specs=[anywhere] * 3,
+        in_specs=[pl.BlockSpec(memory_space=pltpu.VMEM)] * 3,
         out_specs=(anywhere, anywhere),
-        scratch_shapes=[
-            vmem(4, 128, 256), vmem(4, 128, dtype=jnp.int32), vmem(4, 256, 256), vmem(32, 4096), dma((6,)), dma((5,)),
-        ],
-    )(rows.reshape(4, 128, 256), masked_index, grad_prototypes)
+        scratch_shapes=[vmem(4, 256, 256), dma((5,))],
+    )(
+        pltpu.with_memory_space_constraint(rows, pltpu.VMEM),
+        masked_index,
+        pltpu.with_memory_space_constraint(grad_prototypes, pltpu.VMEM),
+    )
 
 
 def solution(mesh):

time: 68.5 us -> 67.7 us (0.988)
  Pallas kernels: 67.8 us -> 66.9 us
where the time goes in v5:
time: 67.7 us; the launch traced here: 67.6 us
  Pallas kernels  66.9 us (99%)
    pallas_call x1, Pallas kernels, body(): pl.pallas_call(kernel, out_shape=(pltpu.VMEM((4, 8, 16, 256), F32), pltpu...  64.9 us
    pallas_call x1, Pallas kernels, body(): pl.pallas_call(place_kernel, out_shape=(jax.ShapeDtypeStruct((1024, 256),...  1.98 us

profile of v5, /device:TPU:1, one launch (start us, length us, event | category | flops | bytes accessed | tf_op | source)
XLA Modules:
  0.0 67.6 jit_solution(17829833392358624372)
XLA Ops:
  0.6 64.9 %shard_map.59 = (f32[4,8,16,256]{3,2,1,0:T(8,128)S(1)}, f32[32,4096]{1,0:T(8,128)S(1)}) custom-call(bf16[1024,256]{1,0:T(8,128)(2,1)} %student_hbm.1, bf16[1024,256]{1,0:T(8,128)(2,1)} %teacher_hbm.1, s32[4,128]{1,0:T(4,128)} %index.1, bf16[256,4096]{1,0:T(8,128)(2,1)} %protos_hbm.1), custom_call_target="tpu_custom_call" | custom-call | tf_op jit(solution)/shard_map/pallas_call | solution.py:573
  65.6 2.0 %shard_map.60 = (f32[1024,256]{1,0:T(8,128)}, f32[32,4096]{1,0:T(8,128)}) custom-call(f32[4,8,16,256]{3,2,1,0:T(8,128)S(1)} %get-tuple-element.4.rows, s32[4,128]{1,0:T(4,128)} %index.1, f32[32,4096]{1,0:T(8,128)S(1)} %get-tuple-element.5.gw), custom_call_target="tpu_custom_call" | custom-call | tf_op jit(solution)/shard_map/pallas_call | solution.py:586

commit v6 on v5

--- a/solution.py
+++ b/solution.py
@@ -52,7 +52,6 @@
     fp, ft, yr, ysum, y_ssem, y_rsem, yp_ssem, yp_rsem, zr, z_ssem, z_rsem,
     ag, agz_ssem, agz_rsem, agy_ssem, agy_rsem,
     gpart, p1r, p1_ssem, p1_rsem, p2r, p2_ssem, p2_rsem,
-    gw_ref, out_sem,
 ):
     dp = lax.axis_index("dp")
     pr = lax.axis_index("proto")
@@ -490,24 +489,25 @@
 
     def finish(j, carry):
         wait_bytes(p2r.at[j], p2_rsem.at[j])
-        gw_ref[j, 0] = gpart[j, block(x, 32 * core, 32), :] + p2r[j, core] + p2r[j, 2 + core]
-        gw_ref[j, 1] = p2r[j, 4] + p2r[j, 1 - core] + p2r[j, 3 - core]
-        for i, start in enumerate((half, 2048 - half)):
-            cols = pl.ds(pl.multiple_of(j * V + start, V), V)
-            pltpu.make_async_copy(gw_ref.at[j, i], gw_hbm.at[:, cols], out_sem.at[0]).start()
+        gw_hbm[:, pl.ds(pl.multiple_of(j * V + half, V), V)] = (
+            gpart[j, block(x, 32 * core, 32), :] + p2r[j, core] + p2r[j, 2 + core]
+        )
+        gw_hbm[:, pl.ds(pl.multiple_of(j * V + 2048 - half, V), V)] = (
+            p2r[j, 4] + p2r[j, 1 - core] + p2r[j, 3 - core]
+        )
         return carry
 
     for dz in (1, 7, 2, 6, 3, 5, 4):
         piece = ag.at[y, lax.rem(z + NZ - dz, NZ)]
         wait_bytes(piece, agz_rsem.at[dz - 1])
         to_y(piece)
-    pltpu.make_async_copy(ag.at[y], rows_hbm.at[y], out_sem.at[1]).start()
+    rows_hbm[y] = ag[y]
     lax.fori_loop(0, 8, finish, 0)
 
     for dy in (1, 3, 2):
         image = lax.rem(y + NY - dy, NY)
         wait_bytes(ag.at[image], agy_rsem.at[dy - 1])
-        pltpu.make_async_copy(ag.at[image], rows_hbm.at[image], out_sem.at[1]).start()
+        rows_hbm[image] = ag[image]
 
     wait_bytes(cbuf.at[:, pl.ds(0, 7)], c_ssem)
     wait_bytes(rbuf.at[:, pl.ds(0, 31)], r_ssem)
@@ -523,8 +523,6 @@
 
     wait_bytes(p1r, p1_ssem)
     wait_bytes(p2r, p2_ssem)
-    wait_bytes(gw_ref, out_sem.at[0])
-    wait_bytes(ag, out_sem.at[1])
 
 
 def place_kernel(rows, index, gw, gp_hbm, gw_hbm, placed, out_sem):
@@ -567,7 +565,7 @@
         vmem(2, 7, 16, 256), dma, dma((2,)),
         vmem(4, 8, 16, 256), dma, dma((7,)), dma, dma((3,)),
         vmem(8, 256, 256), vmem(8, 2, 32, 256), dma, dma((8,)),
-        vmem(8, 5, 32, 256), dma, dma((8,)), vmem(8, 2, 32, 256), dma((2,)),
+        vmem(8, 5, 32, 256), dma, dma((8,)),
     ]
     anywhere = pl.BlockSpec(memory_space=pl.ANY)
     rows, grad_prototypes = pl.pallas_call(
@@ -577,7 +575,7 @@
             pltpu.VMEM((32, 4096), F32),
         ),
         in_specs=[anywhere] * 4,
-        out_specs=(anywhere, anywhere),
+        out_specs=(pl.BlockSpec(memory_space=pltpu.VMEM),) * 2,
         scratch_shapes=scratch,
         compiler_params=pltpu.CompilerParams(
             collective_id=0, has_side_effects=True, vmem_limit_bytes=60 * 1024 * 1024

time: 67.7 us -> 67.2 us (level)
  no operation moved by 1% of the time
where the time goes in v6:
time: 67.2 us; the launch traced here: 67 us
  Pallas kernels  66.4 us (99%)
    pallas_call x1, Pallas kernels, body(): pl.pallas_call(kernel, out_shape=(pltpu.VMEM((4, 8, 16, 256), F32), pltpu...  64.4 us
    pallas_call x1, Pallas kernels, body(): pl.pallas_call(place_kernel, out_shape=(jax.ShapeDtypeStruct((1024, 256),...  1.98 us

profile of v6, /device:TPU:1, one launch (start us, length us, event | category | flops | bytes accessed | tf_op | source)
XLA Modules:
  0.0 67.0 jit_solution(2200660061609177176)
XLA Ops:
  0.6 64.4 %shard_map.59 = (f32[4,8,16,256]{3,2,1,0:T(8,128)S(1)}, f32[32,4096]{1,0:T(8,128)S(1)}) custom-call(bf16[1024,256]{1,0:T(8,128)(2,1)} %student_hbm.1, bf16[1024,256]{1,0:T(8,128)(2,1)} %teacher_hbm.1, s32[4,128]{1,0:T(4,128)} %index.1, bf16[256,4096]{1,0:T(8,128)(2,1)} %protos_hbm.1), custom_call_target="tpu_custom_call" | custom-call | tf_op jit(solution)/shard_map/pallas_call | solution.py:571
  65.0 2.0 %shard_map.60 = (f32[1024,256]{1,0:T(8,128)}, f32[32,4096]{1,0:T(8,128)}) custom-call(f32[4,8,16,256]{3,2,1,0:T(8,128)S(1)} %get-tuple-element.4.rows, s32[4,128]{1,0:T(4,128)} %index.1, f32[32,4096]{1,0:T(8,128)S(1)} %get-tuple-element.5.gw), custom_call_target="tpu_custom_call" | custom-call | tf_op jit(solution)/shard_map/pallas_call | solution.py:584
